TPU v7x, 128 devices: a whole 4x4x4 slice. The times are simulated.
128 devices in a mesh: samp: 16 (over z, x), state: 8 (over y, core).
Axes of the slice: x: 4, y: 4, z: 4, core: 2. Of those that a mesh axis runs over, the one named last changes fastest.
Arguments:
- energies: bfloat16 [4096, 262144], P('state', 'samp'), may hold values from -12 to 12
- offsets: float32 [4096, 2048], P('state', 'samp'), may hold values from -250 to 250
- counts: int32 [4096], P('state'), may hold values from 1 to 64513, as said below
- labels: int32 [262144], P('samp'), may hold values from 0 to 4095
Outputs:
- free_energy: float32 [4096], P('state')
- own_log_probability: float32 [262144], P('samp')
Inputs may be any that keep to these rules, and one draw needn't show every extreme that they name: counts[k] is the number of samples n with labels[n] = k; every state has a sample, state 4096 - 1 has exactly one, and state 0 has the most.
All inputs are finite; a program needn't handle non-finite values.
Results may differ from a plain program's by a relative error of at most 0.0003.
Values sent between devices are 32-bit elements; how exact they have to be, the bound alone decides.
No kernel may reach another device: no remote copies, remote signals or barrier semaphores. Data moves between devices by JAX's collectives and lax.ppermute only.
A program may use at most 192 MiB of HBM per device.

v0:
```python
import jax
import jax.numpy as jnp
from jax import lax
from jax.sharding import PartitionSpec as P

ITERS = 3


def from_root(value, axis, root):
    mine = lax.axis_index(axis) == root
    return lax.psum(jnp.where(mine, value, jnp.zeros_like(value)), axis)


def local_energy(energies, offsets):
    rows, width = energies.shape
    nblk = offsets.shape[1]
    shaped = energies.astype(jnp.float32).reshape(rows, nblk, width // nblk)
    return (shaped + offsets[:, :, None]).reshape(rows, width)


def sample_denominator(energies, offsets, lead):
    terms = lead[:, None] - local_energy(energies, offsets)
    best = lax.pmax(jnp.max(terms, axis=0), "state")
    total = lax.psum(jnp.sum(jnp.exp(terms - best[None, :]), axis=0), "state")
    return best + jnp.log(total)


def state_update(energies, offsets, denom):
    terms = -local_energy(energies, offsets) - denom[None, :]
    best = lax.pmax(jnp.max(terms, axis=1), "samp")
    total = lax.psum(jnp.sum(jnp.exp(terms - best[:, None]), axis=1), "samp")
    return -(best + jnp.log(total))


def own_terms_local(energies, offsets, lead, local_label):
    rows, width = energies.shape
    nblk = offsets.shape[1]
    block_size = width // nblk
    span = min(width, max(block_size, 512))
    span = span - span % block_size
    while width % span != 0:
        span = span - block_size
    steps_count = width // span
    row_ids = jnp.arange(rows, dtype=jnp.int32)

    def one(index):
        start = index * span
        part = lax.dynamic_slice_in_dim(energies, start, span, 1).astype(jnp.float32)
        shift = lax.dynamic_slice_in_dim(
            offsets, index * (span // block_size), span // block_size, 1
        )
        energy_part = (
            part.reshape(rows, span // block_size, block_size) + shift[:, :, None]
        ).reshape(rows, span)
        wanted = lax.dynamic_slice_in_dim(local_label, start, span, 0)
        match = row_ids[:, None] == wanted[None, :]
        return jnp.sum(jnp.where(match, lead[:, None] - energy_part, 0.0), axis=0)

    return lax.map(one, jnp.arange(steps_count, dtype=jnp.int32)).reshape(width)


def shards(energies, offsets, counts, labels):
    rows, width = energies.shape
    logc = jnp.log(counts.astype(jnp.float32))
    free = jnp.zeros((rows,), jnp.float32)
    for step in range(ITERS):
        denom = sample_denominator(energies, offsets, logc + free)
        free = state_update(energies, offsets, denom)
    lead = logc + free
    denom = sample_denominator(energies, offsets, lead)
    local_label = labels - lax.axis_index("state") * rows
    picked = own_terms_local(energies, offsets, lead, local_label)
    own = lax.psum(picked, "state") - denom
    anchor_value = from_root(free[0:1], "state", 0)
    return (free - anchor_value[0], own)


def solution(mesh):
    return jax.shard_map(
        shards,
        mesh=mesh,
        in_specs=(P("state", "samp"), P("state", "samp"), P("state"), P("samp")),
        out_specs=(P("state"), P("samp")),
        check_vma=False,
    )
```

profile of v0, /device:TPU:1, one launch (start us, length us, event | category | flops | bytes accessed | tf_op | source)
XLA Modules:
  0.0 1031.4 jit_solution(1025011676120550633)
XLA Ops:
  8.1 15.3 %add.56 = f32[512,128,128]{2,1,0:T(8,128)} broadcast(f32[512,128]{1,0:T(8,128)} %param.7), dimensions={0,1} | broadcast | bytes 33816576 | tf_op jit(solution)/shard_map/add | solution.py:18
  23.4 38.4 %subtract_reduce_fusion.6 = (f32[16384]{0:T(1024)}, f32[512,16384]{1,0:T(8,128)}) fusion(f32[512]{0:T(512)S(1)} %convert_log_fusion, f32[64,8,128,128]{3,2,1,0:T(8,128)} %bitcast.30, bf16[512,16384]{1,0:T(8,128)(2,1)S(1)} %bitcast.33), kind=kLoop, calls=%fused_computation.21 | loop fusion | flops 33538048 | bytes 83953664 | tf_op jit(solution)/shard_map/reduce_max | solution.py:23
  61.9 60.0 %all-reduce.10.cloned.1.call-done = f32[16384]{0:T(1024)} async-done(((f32[16384]{0:T(1024)}), f32[16384]{0:T(1024)}) %all-reduce.10.cloned.1.call-update) | async-done | bytes 65552 | tf_op jit(solution)/shard_map/pmax | solution.py:23
  121.9 16.1 %exponential_reduce_fusion.6 = f32[16384]{0:T(1024)} fusion(f32[512,16384]{1,0:T(8,128)} %get-tuple-element.80, f32[16384]{0:T(1024)} %all-reduce.10.cloned.1.call-done, f32[512]{0:T(512)S(1)} %convert_log_fusion), kind=kLoop, calls=%fused_computation.14 | loop fusion | flops 25149440 | bytes 33687552 | tf_op jit(solution)/shard_map/reduce_sum | solution.py:24
  138.0 57.9 %all-reduce.12.cloned.1.call-done = f32[16384]{0:T(1024)} async-done(((f32[16384]{0:T(1024)}), f32[16384]{0:T(1024)}) %all-reduce.12.cloned.1.call-update) | async-done | bytes 65552 | tf_op jit(solution)/shard_map/psum | solution.py:24
  196.8 12.8 %subtract_reduce_fusion.5 = f32[512]{0:T(512)S(1)} fusion(f32[512,16384]{1,0:T(8,128)} %get-tuple-element.80, f32[16384]{0:T(1024)S(1)} %log_add_fusion.2), kind=kLoop, calls=%fused_computation.20 | loop fusion | flops 25165312 | bytes 33622016 | tf_op jit(solution)/shard_map/reduce_max | solution.py:30
  209.6 33.5 %pmax.50 = f32[512]{0:T(512)S(1)} all-reduce(f32[512]{0:T(512)S(1)} %subtract_reduce_fusion.5), channel_id=1, replica_groups=mesh['samp'=16,'state'=8] {'samp'}, use_global_device_ids=true, to_apply=%region_5.0 | all-reduce | flops 512 | bytes 4096 | tf_op jit(solution)/shard_map/pmax | solution.py:30
  243.1 14.5 %exponential_reduce_fusion.5 = f32[512]{0:T(512)S(1)} fusion(f32[512,16384]{1,0:T(8,128)} %get-tuple-element.80, f32[512]{0:T(512)S(1)} %pmax.50, f32[16384]{0:T(1024)S(1)} %log_add_fusion.2), kind=kLoop, calls=%fused_computation.13 | loop fusion | flops 33553920 | bytes 33624064 | tf_op jit(solution)/shard_map/reduce_sum | solution.py:31
  257.7 28.6 %psum.64 = f32[512]{0:T(512)S(1)} all-reduce(f32[512]{0:T(512)S(1)} %exponential_reduce_fusion.5), channel_id=1, replica_groups=mesh['samp'=16,'state'=8] {'samp'}, use_global_device_ids=true, to_apply=%region_7.0 | all-reduce | flops 512 | bytes 4096 | tf_op jit(solution)/shard_map/psum | solution.py:31
  286.2 13.2 %subtract_reduce_fusion.4 = f32[16384]{0:T(1024)} fusion(f32[512,16384]{1,0:T(8,128)} %get-tuple-element.80, f32[512]{0:T(512)S(1)} %negate_add_fusion.1), kind=kLoop, calls=%fused_computation.19 | loop fusion | flops 16760832 | bytes 33622016 | tf_op jit(solution)/shard_map/reduce_max | solution.py:23
  299.5 68.0 %all-reduce.14.cloned.1.call-done = f32[16384]{0:T(1024)} async-done(((f32[16384]{0:T(1024)}), f32[16384]{0:T(1024)}) %all-reduce.14.cloned.1.call-update) | async-done | bytes 65552 | tf_op jit(solution)/shard_map/pmax | solution.py:23
  367.5 16.1 %exponential_reduce_fusion.4 = f32[16384]{0:T(1024)} fusion(f32[512,16384]{1,0:T(8,128)} %get-tuple-element.80, f32[16384]{0:T(1024)} %all-reduce.14.cloned.1.call-done, f32[512]{0:T(512)S(1)} %negate_add_fusion.1), kind=kLoop, calls=%fused_computation.12 | loop fusion | flops 25149440 | bytes 33687552 | tf_op jit(solution)/shard_map/reduce_sum | solution.py:24
  383.7 57.9 %all-reduce.16.cloned.1.call-done = f32[16384]{0:T(1024)} async-done(((f32[16384]{0:T(1024)}), f32[16384]{0:T(1024)}) %all-reduce.16.cloned.1.call-update) | async-done | bytes 65552 | tf_op jit(solution)/shard_map/psum | solution.py:24
  442.5 12.8 %subtract_reduce_fusion.3 = f32[512]{0:T(512)S(1)} fusion(f32[512,16384]{1,0:T(8,128)} %get-tuple-element.80, f32[16384]{0:T(1024)S(1)} %log_add_fusion.1), kind=kLoop, calls=%fused_computation.18 | loop fusion | flops 25165312 | bytes 33622016 | tf_op jit(solution)/shard_map/reduce_max | solution.py:30
  455.3 33.5 %pmax.52 = f32[512]{0:T(512)S(1)} all-reduce(f32[512]{0:T(512)S(1)} %subtract_reduce_fusion.3), channel_id=1, replica_groups=mesh['samp'=16,'state'=8] {'samp'}, use_global_device_ids=true, to_apply=%region_13.0 | all-reduce | flops 512 | bytes 4096 | tf_op jit(solution)/shard_map/pmax | solution.py:30
  488.8 14.5 %exponential_reduce_fusion.3 = f32[512]{0:T(512)S(1)} fusion(f32[512,16384]{1,0:T(8,128)} %get-tuple-element.80, f32[512]{0:T(512)S(1)} %pmax.52, f32[16384]{0:T(1024)S(1)} %log_add_fusion.1), kind=kLoop, calls=%fused_computation.11 | loop fusion | flops 33553920 | bytes 33624064 | tf_op jit(solution)/shard_map/reduce_sum | solution.py:31
  503.3 28.6 %psum.66 = f32[512]{0:T(512)S(1)} all-reduce(f32[512]{0:T(512)S(1)} %exponential_reduce_fusion.3), channel_id=1, replica_groups=mesh['samp'=16,'state'=8] {'samp'}, use_global_device_ids=true, to_apply=%region_15.0 | all-reduce | flops 512 | bytes 4096 | tf_op jit(solution)/shard_map/psum | solution.py:31
  531.9 13.2 %subtract_reduce_fusion.2 = f32[16384]{0:T(1024)} fusion(f32[512,16384]{1,0:T(8,128)} %get-tuple-element.80, f32[512]{0:T(512)S(1)} %negate_add_fusion), kind=kLoop, calls=%fused_computation.17 | loop fusion | flops 16760832 | bytes 33622016 | tf_op jit(solution)/shard_map/reduce_max | solution.py:23
  545.4 67.8 %all-reduce.18.cloned.1.call-done = f32[16384]{0:T(1024)} async-done(((f32[16384]{0:T(1024)}), f32[16384]{0:T(1024)}) %all-reduce.18.cloned.1.call-update) | async-done | bytes 65552 | tf_op jit(solution)/shard_map/pmax | solution.py:23
  613.2 16.1 %exponential_reduce_fusion.2 = f32[16384]{0:T(1024)} fusion(f32[512,16384]{1,0:T(8,128)} %get-tuple-element.80, f32[16384]{0:T(1024)} %all-reduce.18.cloned.1.call-done, f32[512]{0:T(512)S(1)} %negate_add_fusion), kind=kLoop, calls=%fused_computation.10 | loop fusion | flops 25149440 | bytes 33687552 | tf_op jit(solution)/shard_map/reduce_sum | solution.py:24
  629.4 57.9 %all-reduce.20.cloned.1.call-done = f32[16384]{0:T(1024)} async-done(((f32[16384]{0:T(1024)}), f32[16384]{0:T(1024)}) %all-reduce.20.cloned.1.call-update) | async-done | bytes 65552 | tf_op jit(solution)/shard_map/psum | solution.py:24
  688.2 12.8 %subtract_reduce_fusion.1 = f32[512]{0:T(512)S(1)} fusion(f32[512,16384]{1,0:T(8,128)} %get-tuple-element.80, f32[16384]{0:T(1024)S(1)} %log_add_fusion), kind=kLoop, calls=%fused_computation.16 | loop fusion | flops 25165312 | bytes 33622016 | tf_op jit(solution)/shard_map/reduce_max | solution.py:30
  700.9 33.5 %pmax.54 = f32[512]{0:T(512)S(1)} all-reduce(f32[512]{0:T(512)S(1)} %subtract_reduce_fusion.1), channel_id=1, replica_groups=mesh['samp'=16,'state'=8] {'samp'}, use_global_device_ids=true, to_apply=%region_21.0 | all-reduce | flops 512 | bytes 4096 | tf_op jit(solution)/shard_map/pmax | solution.py:30
  734.5 14.6 %exponential_reduce_fusion.1 = f32[512]{0:T(512)S(1)} fusion(f32[512,16384]{1,0:T(8,128)} %get-tuple-element.80, f32[512]{0:T(512)S(1)} %pmax.54, f32[16384]{0:T(1024)S(1)} %log_add_fusion), kind=kLoop, calls=%fused_computation.9 | loop fusion | flops 33553920 | bytes 33624064 | tf_op jit(solution)/shard_map/reduce_sum | solution.py:31
  749.1 28.6 %psum.68 = f32[512]{0:T(512)S(1)} all-reduce(f32[512]{0:T(512)S(1)} %exponential_reduce_fusion.1), channel_id=1, replica_groups=mesh['samp'=16,'state'=8] {'samp'}, use_global_device_ids=true, to_apply=%region_23.0 | all-reduce | flops 512 | bytes 4096 | tf_op jit(solution)/shard_map/psum | solution.py:31
  777.6 13.2 %subtract_reduce_fusion = f32[16384]{0:T(1024)} fusion(f32[512,16384]{1,0:T(8,128)} %get-tuple-element.80, f32[512]{0:T(512)S(1)} %get-tuple-element.128), kind=kLoop, calls=%fused_computation.15 | loop fusion | flops 16760832 | bytes 33622016 | tf_op jit(solution)/shard_map/reduce_max | solution.py:23
  790.9 131.9 %while.11 = (s32[]{:T(128)}, f32[32,512]{1,0:T(8,128)S(1)}, s32[32]{0:T(128)S(1)}, s32[16384]{0:T(1024)S(1)}, f32[512]{0:T(512)S(1)}, /*index=5*/bf16[512,16384]...) while((s32[]{:T(128)}, f32[32,512]{1,0:T(8,128)S(1)}, ...), condition=%wide.region_27.0_spmd.clone, body=%wide.region_25.27_spmd.clone.sunk | while | flops 1572362 | bytes 2660597 | solution.py:59
  793.7 1.3 fusion.7
  797.8 1.3 fusion.7
  801.9 1.3 fusion.7
  806.0 1.3 fusion.7
  810.1 1.3 fusion.7
  814.3 1.3 fusion.7
  818.4 1.3 fusion.7
  822.5 1.3 fusion.7
  826.6 1.3 fusion.7
  830.8 1.3 fusion.7
  834.9 1.3 fusion.7
  839.0 1.3 fusion.7
  843.1 1.3 fusion.7
  847.3 1.3 fusion.7
  851.4 1.3 fusion.7
  855.5 1.3 fusion.7
  859.6 1.3 fusion.7
  863.7 1.3 fusion.7
  867.9 1.3 fusion.7
  872.0 1.3 fusion.7
  876.1 1.3 fusion.7
  880.2 1.3 fusion.7
  884.4 1.3 fusion.7
  888.5 1.3 fusion.7
  892.6 1.3 fusion.7
  896.7 1.3 fusion.7
  900.8 1.3 fusion.7
  905.0 1.3 fusion.7
  909.1 1.3 fusion.7
  913.2 1.3 fusion.7
  917.3 1.3 fusion.7
  921.5 1.3 fusion.7
  924.0 29.6 %psum.69 = f32[]{:T(128)} all-reduce(f32[]{:T(128)} %bitcast.1), channel_id=1, replica_groups=mesh['samp'=16,'state'=8] {'state'}, use_global_device_ids=true, to_apply=%region_24.0 | all-reduce | flops 1 | bytes 8 | tf_op jit(solution)/shard_map/psum | solution.py:11
  954.2 16.1 %exponential_reduce_fusion = f32[16384]{0:T(1024)} fusion(f32[512,16384]{1,0:T(8,128)} %get-tuple-element.80, f32[16384]{0:T(1024)} %all-reduce.22.cloned.1.call-done, f32[512]{0:T(512)S(1)} %get-tuple-element.195), kind=kLoop, calls=%fused_computation.8 | loop fusion | flops 25149440 | bytes 33687552 | tf_op jit(solution)/shard_map/reduce_sum | solution.py:24
  970.4 1.1 broadcast_subtract_fusion.1
  971.5 51.6 %all-reduce.24.cloned.1.call-done = (f32[16384]{0:T(1024)}, f32[16384]{0:T(1024)}) async-done(((f32[16384]{0:T(1024)}, f32[16384]{0:T(1024)}), (f32[16384]{0:T(1024)}, f32[16384]{0:T(1024)})) %all-reduce.24.cloned.1.call-update) | async-done | bytes 131088 | tf_op jit(solution)/shard_map/psum | solution.py:73
  1023.1 1.5 add_subtract_fusion
  (212 shorter events, 51.9 us)
Async XLA Ops:
  7.2 114.7 %all-reduce.10.cloned.1.call-start = ((), (), s32[]{:S(2)}) async-start(), calls=%async_computation | async-start | bytes 131072 | tf_op jit(solution)/shard_map/pmax | solution.py:23
  7.2 16.2 %slice-start = ((s8[16777216]{0:T(1024)(128)(4,1)}), s8[4194304]{0:T(1024)(128)(4,1)S(1)}, s32[]{:S(2)}) async-start(s8[16777216]{0:T(1024)(128)(4,1)} %bitcast.32), calls=%async_computation.8 | async-start | bytes 8388608
  8.1 15.3 %slice-start.1 = ((s8[16777216]{0:T(1024)(128)(4,1)}), s8[4194304]{0:T(1024)(128)(4,1)S(1)}, s32[]{:S(2)}) async-start(s8[16777216]{0:T(1024)(128)(4,1)} %bitcast.32), calls=%async_computation.9 | async-start | bytes 8388608
  8.1 15.3 %slice-start.2 = ((s8[16777216]{0:T(1024)(128)(4,1)}), s8[4194304]{0:T(1024)(128)(4,1)S(1)}, s32[]{:S(2)}) async-start(s8[16777216]{0:T(1024)(128)(4,1)} %bitcast.32), calls=%async_computation.10 | async-start | bytes 8388608
  8.1 15.3 %slice-start.3 = ((s8[16777216]{0:T(1024)(128)(4,1)}), s8[4194304]{0:T(1024)(128)(4,1)S(1)}, s32[]{:S(2)}) async-start(s8[16777216]{0:T(1024)(128)(4,1)} %bitcast.32), calls=%async_computation.11 | async-start | bytes 8388608
  61.8 134.1 %all-reduce.12.cloned.1.call-start = ((), (), s32[]{:S(2)}) async-start(), calls=%async_computation.1 | async-start | bytes 131072 | tf_op jit(solution)/shard_map/psum | solution.py:24
  121.9 74.1 %copy-start.2 = (f32[16384]{0:T(1024)S(1)}, f32[16384]{0:T(1024)}, u32[]{:S(2)}) copy-start(f32[16384]{0:T(1024)} %all-reduce.10.cloned.1.call-done) | copy-start | bytes 196612
  138.0 229.5 %all-reduce.14.cloned.1.call-start = ((), (), s32[]{:S(2)}) async-start(), calls=%async_computation.2 | async-start | bytes 131072 | tf_op jit(solution)/shard_map/pmax | solution.py:23
  196.8 89.4 %copy-start.6 = (s32[512]{0:T(512)S(1)}, s32[512]{0:T(512)}, u32[]{:S(2)}) copy-start(s32[512]{0:T(512)} %param.8) | copy-start | bytes 6148
  299.5 142.1 %all-reduce.16.cloned.1.call-start = ((), (), s32[]{:S(2)}) async-start(), calls=%async_computation.3 | async-start | bytes 131072 | tf_op jit(solution)/shard_map/psum | solution.py:24
  367.5 74.1 %copy-start.3 = (f32[16384]{0:T(1024)S(1)}, f32[16384]{0:T(1024)}, u32[]{:S(2)}) copy-start(f32[16384]{0:T(1024)} %all-reduce.14.cloned.1.call-done) | copy-start | bytes 196612
  383.7 229.6 %all-reduce.18.cloned.1.call-start = ((), (), s32[]{:S(2)}) async-start(), calls=%async_computation.4 | async-start | bytes 131072 | tf_op jit(solution)/shard_map/pmax | solution.py:23
  531.9 97.5 %copy-start.5 = (s32[16384]{0:T(1024)S(1)}, s32[16384]{0:T(1024)}, u32[]{:S(2)}) copy-start(s32[16384]{0:T(1024)} %param.9) | copy-start | bytes 196612
  545.2 142.1 %all-reduce.20.cloned.1.call-start = ((), (), s32[]{:S(2)}) async-start(), calls=%async_computation.5 | async-start | bytes 131072 | tf_op jit(solution)/shard_map/psum | solution.py:24
  613.2 74.1 %copy-start.1 = (f32[16384]{0:T(1024)S(1)}, f32[16384]{0:T(1024)}, u32[]{:S(2)}) copy-start(f32[16384]{0:T(1024)} %all-reduce.18.cloned.1.call-done) | copy-start | bytes 196612
  629.3 324.9 %all-reduce.22.cloned.1.call-start = ((), (), s32[]{:S(2)}) async-start(), calls=%async_computation.6 | async-start | bytes 131072 | tf_op jit(solution)/shard_map/pmax | solution.py:23
  734.5 56.5 %copy-start = (f32[512,128]{1,0:T(8,128)S(1)}, f32[512,128]{1,0:T(8,128)}, u32[]{:S(2)}) copy-start(f32[512,128]{1,0:T(8,128)} %param.7) | copy-start | bytes 786436
  790.9 232.2 %all-reduce.24.cloned.1.call-start = ((), (), s32[]{:S(2)}) async-start(), calls=%async_computation.7 | async-start | bytes 262144 | tf_op jit(solution)/shard_map/psum | solution.py:73
  954.2 68.8 %copy-start.4 = (f32[16384]{0:T(1024)S(1)}, f32[16384]{0:T(1024)}, u32[]{:S(2)}) copy-start(f32[16384]{0:T(1024)} %all-reduce.22.cloned.1.call-done) | copy-start | bytes 196612
Sparse Core Ops, SparseCore 0:
  61.9 59.8 all-reduce.9
  138.1 57.7 all-reduce.11
  299.6 67.8 all-reduce.13
  383.8 57.7 all-reduce.15
  545.3 67.8 all-reduce.17
  629.5 57.7 all-reduce.19
  791.0 68.0 all-reduce.21
  970.5 52.5 all-reduce.23
where the time goes:
time: 1040 us; the launch traced here: 1030 us
  waiting for transfers between devices  421 us (40%)
  other arithmetic  273 us (26%)
  blocking collectives  216 us (21%)
  local copies, waits for them, and re-layouts  63.2 us (6%)
  loops' own time  43.2 us (4%)
  between operations  14.9 us (1%)
    pmax x4, waiting for transfers between devices, sample_denominator(): best = lax.pmax(jnp.max(terms, axis=0), 'state')  196 us
    psum x3, waiting for transfers between devices, sample_denominator(): total = lax.psum(jnp.sum(jnp.exp(terms - best[None, :]), axis=0), 'state')  174 us
    pmax x3, blocking collectives, state_update(): best = lax.pmax(jnp.max(terms, axis=1), 'samp')  101 us
    psum x3, blocking collectives, state_update(): total = lax.psum(jnp.sum(jnp.exp(terms - best[:, None]), axis=1), 'samp')  85.7 us
    reduce_max x4, other arithmetic, sample_denominator(): best = lax.pmax(jnp.max(terms, axis=0), 'state')  78 us
    reduce_sum x4, other arithmetic, sample_denominator(): total = lax.psum(jnp.sum(jnp.exp(terms - best[None, :]), axis=0), 'state')  64.4 us
    psum x1, waiting for transfers between devices, shards(): own = lax.psum(picked, 'state') - denom  51.6 us
    reduce_sum x3, other arithmetic, state_update(): total = lax.psum(jnp.sum(jnp.exp(terms - best[:, None]), axis=1), 'samp')  43.7 us
  transfers between devices with their start and end apart: 8, of which 7 were waited for; matrix products, arithmetic and copies ran while one was open for 9% of the time, Pallas kernels for 0%

commit v1 on v0

v1 whole, which is shorter than its diff:
```python
import functools

import jax
import jax.numpy as jnp
from jax import lax
from jax.experimental import pallas as pl
from jax.experimental.pallas import tpu as pltpu
from jax.sharding import PartitionSpec as P

ITERS = 3
LANES = 128
GROUP = 8
PIECES = 2
VMEM = pltpu.VMEM
WHOLE = pl.BlockSpec(memory_space=pltpu.VMEM)


def params(mib):
    return pltpu.CompilerParams(vmem_limit_bytes=mib << 20)


def block_weights(lead, offt_ref, w_ref, top_ref):
    h = lead - offt_ref[...]
    top = jnp.max(h, axis=1, keepdims=True)
    top_ref[...] = jnp.broadcast_to(top, top_ref.shape)
    w_ref[...] = jnp.exp(h - top)


def spread(ref, g, j, q):
    tile = ref[pl.ds(pl.multiple_of(g * GROUP, GROUP), GROUP), q * LANES : (q + 1) * LANES]
    return jnp.broadcast_to(tile[j : j + 1, :], (8, LANES))


def row_sums(load, w_ref, g, j, acc, rows):
    lane = lax.broadcasted_iota(jnp.int32, (8, acc[0].shape[1]), 1)
    here = lane == g * GROUP + j
    nq = w_ref.shape[1] // LANES
    w = [spread(w_ref, g, j, q) for q in range(nq)]
    out = []
    for i in range(rows // 8):
        total = load(i, 0) * w[0]
        for q in range(1, nq):
            total = total + load(i, q) * w[q]
        col = jnp.sum(total, axis=1, keepdims=True)
        out.append(jnp.where(here, col, acc[i]))
    return tuple(out)


def log_rows(acc, top_ref):
    return top_ref[...] + jnp.log(jnp.concatenate(acc, axis=0).T)


def over_pieces(step, ex_refs, steps, carry):
    each = steps // len(ex_refs)
    for p, ex_ref in enumerate(ex_refs):
        carry = lax.fori_loop(p * each, (p + 1) * each, functools.partial(step, ex_ref, p * each), carry)
    return carry


def prep_kernel(e_hbm, off_ref, counts_ref, labels_ref, mine_ref, *refs):
    ex_refs, (offt_ref, out_ref, local_ref, root_ref, buf, sem, w_ref, top_ref) = refs[:PIECES], refs[PIECES:]
    rows = LANES
    nk = buf.shape[1]
    nq = nk // LANES
    span = buf.shape[2]
    steps = e_hbm.shape[1] // span

    def copy(step, slot):
        at = pl.multiple_of(step * span, span)
        return pltpu.make_async_copy(e_hbm.at[:, pl.ds(at, span)], buf.at[slot], sem.at[slot])

    copy(0, 0).start()
    mine = mine_ref[...]
    local_ref[...] = labels_ref[...] - mine * nk
    root_ref[...] = (mine == 0).astype(jnp.int32)
    offt_ref[...] = off_ref[...].T
    block_weights(jnp.log(counts_ref[...].astype(jnp.float32)), offt_ref, w_ref, top_ref)

    def step(ex_ref, first, g, acc):
        slot = lax.rem(g, 2)

        @pl.when(g + 1 < steps)
        def _():
            copy(g + 1, 1 - slot).start()

        copy(g, slot).wait()
        for j in range(span // rows):
            base = pl.multiple_of((g - first) * span + j * rows, rows)
            for q in range(nq):
                tile = buf[slot, q * LANES : (q + 1) * LANES, j * rows : (j + 1) * rows]
                ex_ref[pl.ds(base, rows), q * LANES : (q + 1) * LANES] = jnp.exp(
                    -(tile.astype(jnp.float32).T)
                )

            def load(i, q, base=base):
                return ex_ref[pl.ds(base + i * 8, 8), q * LANES : (q + 1) * LANES]

            acc = row_sums(load, w_ref, g, j, acc, rows)
        return acc

    acc = (jnp.zeros((8, out_ref.shape[0]), jnp.float32),) * (rows // 8)
    acc = over_pieces(step, ex_refs, steps, acc)
    out_ref[...] = log_rows(acc, top_ref)


def prep(energies, offsets, counts, labels, mine):
    nk, width = energies.shape
    nblk = offsets.shape[1]
    span = GROUP * LANES
    return pl.pallas_call(
        prep_kernel,
        out_shape=(pltpu.VMEM((width // PIECES, nk), jnp.float32),) * PIECES + (
            jax.ShapeDtypeStruct((nblk, nk), jnp.float32),
            jax.ShapeDtypeStruct((nblk, LANES), jnp.float32),
            jax.ShapeDtypeStruct(labels.shape, jnp.int32),
            jax.ShapeDtypeStruct((1, 1), jnp.int32),
        ),
        in_specs=[pl.BlockSpec(memory_space=pl.ANY)] + [WHOLE] * 4,
        out_specs=(WHOLE,) * (PIECES + 4),
        scratch_shapes=[
            pltpu.VMEM((2, nk, span), jnp.bfloat16),
            pltpu.SemaphoreType.DMA((2,)),
            pltpu.VMEM((nblk, nk), jnp.float32),
            pltpu.VMEM((nblk, LANES), jnp.float32),
        ],
        compiler_params=params(12),
        name="prep",
    )(energies, offsets, counts, labels, mine)


def pick_kernel(e_ref, label_ref, _, out_ref):
    nk, span = e_ref.shape
    kid = lax.broadcasted_iota(jnp.int32, (16, LANES), 0)
    for j in range(span // LANES):
        want = jnp.broadcast_to(label_ref[j : j + 1, :], (16, LANES))
        acc = jnp.zeros((16, LANES), jnp.float32)
        for k in range(nk // 16):
            tile = e_ref[k * 16 : (k + 1) * 16, j * LANES : (j + 1) * LANES].astype(jnp.float32)
            acc = jnp.where(want == kid + k * 16, tile, acc)
        out_ref[j : j + 1, :] = jnp.sum(acc, axis=0, keepdims=True)


def pick(energies, local_label, after):
    nk, width = energies.shape
    span = GROUP * LANES
    return pl.pallas_call(
        pick_kernel,
        grid=(width // span,),
        out_shape=jax.ShapeDtypeStruct(local_label.shape, jnp.float32),
        in_specs=[
            pl.BlockSpec((nk, span), lambda i: (0, i)),
            pl.BlockSpec((GROUP, LANES), lambda i: (i, 0)),
            pl.BlockSpec(memory_space=pl.ANY),
        ],
        out_specs=pl.BlockSpec((GROUP, LANES), lambda i: (i, 0)),
        compiler_params=params(8),
        cost_estimate=pl.CostEstimate(flops=width * nk * 3, bytes_accessed=width * nk * 2, transcendentals=0),
        name="pick",
    )(pltpu.with_memory_space_constraint(energies, pltpu.HBM), local_label, after)


def lse(values):
    best = functools.reduce(jnp.maximum, values)
    return best + jnp.log(sum(jnp.exp(v - best) for v in values))


def update_kernel(n_in, *refs):
    parts, ex_refs, offt_ref = refs[:n_in], refs[n_in : n_in + PIECES], refs[n_in + PIECES]
    out_ref, vt_ref, g_ref = refs[-3:]
    nblk, nk = offt_ref.shape
    nq = nk // LANES
    d = lse([p[...] for p in parts])
    low = jnp.min(d, axis=1, keepdims=True)
    vt_ref[...] = jnp.exp(low - d).T
    h = -offt_ref[...] - low
    top = jnp.max(h, axis=0, keepdims=True)
    g_ref[...] = jnp.exp(h - top)

    def step(ex_ref, first, g, total):
        cols = [
            pltpu.roll(vt_ref[i * 8 : (i + 1) * 8, :], lax.rem(nblk - g * GROUP, nblk), 1)
            for i in range(LANES // 8)
        ]
        for j in range(GROUP):
            acc = [None] * nq
            for i in range(LANES // 8):
                v = jnp.broadcast_to(cols[i][:, j : j + 1], (8, LANES))
                at = pl.multiple_of(((g - first) * GROUP + j) * LANES + i * 8, 8)
                for q in range(nq):
                    term = ex_ref[pl.ds(at, 8), q * LANES : (q + 1) * LANES] * v
                    acc[q] = term if acc[q] is None else acc[q] + term
            total = tuple(
                total[q] + acc[q] * spread(g_ref, g, j, q)
                for q in range(nq)
            )
        return total

    zero = jnp.zeros((8, LANES), jnp.float32)
    total = over_pieces(step, ex_refs, nblk // GROUP, (zero,) * nq)
    sums = jnp.concatenate([jnp.sum(t, axis=0, keepdims=True) for t in total], axis=1)
    out_ref[...] = jnp.broadcast_to((top + jnp.log(sums))[None], out_ref.shape)


def update(parts, ex, offt, copies, after=()):
    nblk, nk = offt.shape
    return pl.pallas_call(
        functools.partial(update_kernel, len(parts)),
        out_shape=jax.ShapeDtypeStruct((copies, 1, nk), jnp.float32),
        in_specs=[WHOLE] * (len(parts) + PIECES + 1) + [pl.BlockSpec(memory_space=pl.ANY)] * len(after),
        out_specs=WHOLE,
        scratch_shapes=[pltpu.VMEM((LANES, nblk), jnp.float32), pltpu.VMEM((nblk, nk), jnp.float32)],
        compiler_params=params(8),
        name="update",
    )(*parts, *(pltpu.with_memory_space_constraint(e, VMEM) for e in ex), offt, *after)


def denom_sums(free, counts_ref, ex_refs, offt_ref, w_ref, top_ref):
    nblk = offt_ref.shape[0]
    lead = jnp.log(counts_ref[...].astype(jnp.float32)) + free
    block_weights(lead, offt_ref, w_ref, top_ref)

    def step(ex_ref, first, g, acc):
        for j in range(GROUP):

            def load(i, q, j=j):
                at = pl.multiple_of(((g - first) * GROUP + j) * LANES + i * 8, 8)
                return ex_ref[pl.ds(at, 8), q * LANES : (q + 1) * LANES]

            acc = row_sums(load, w_ref, g, j, acc, LANES)
        return acc

    acc = (jnp.zeros((8, nblk), jnp.float32),) * (LANES // 8)
    acc = over_pieces(step, ex_refs, nblk // GROUP, acc)
    return lead, log_rows(acc, top_ref)


def free_of(gathered):
    best = jnp.max(gathered, axis=0, keepdims=True)
    total = jnp.sum(jnp.exp(gathered - best), axis=0, keepdims=True)
    return -(best + jnp.log(total))[0]


def denom_kernel(gathered_ref, counts_ref, *refs):
    ex_refs, (offt_ref, out_ref, w_ref, top_ref) = refs[:PIECES], refs[PIECES:]
    free = free_of(gathered_ref[...])
    out_ref[...] = denom_sums(free, counts_ref, ex_refs, offt_ref, w_ref, top_ref)[1]


def last_kernel(gathered_ref, counts_ref, *refs):
    ex_refs, (offt_ref, label_ref, picked_ref, root_ref, out_ref, free_ref, w_ref, top_ref) = refs[:PIECES], refs[PIECES:]
    nblk, nk = offt_ref.shape
    free = free_of(gathered_ref[...])
    free_ref[...] = free
    lead, sums = denom_sums(free, counts_ref, ex_refs, offt_ref, w_ref, top_ref)
    out_ref[0:nblk, :] = sums
    for r in range(nblk // 8):
        at = slice(r * 8, (r + 1) * 8)
        label = label_ref[at, :]
        low = label & (LANES - 1)
        high = label >> 7
        own = jnp.zeros((8, LANES), jnp.float32)
        for q in range(nk // LANES):
            cut = slice(q * LANES, (q + 1) * LANES)
            table = lead[:, cut] - offt_ref[at, cut]
            value = jnp.take_along_axis(table, low, axis=1, mode="promise_in_bounds")
            own = jnp.where(high == q, value - picked_ref[at, :], own)
        out_ref[nblk + r * 8 : nblk + (r + 1) * 8, :] = own
    anchor = jnp.where(root_ref[...] == 1, free[0:1, 0:1], 0.0)
    out_ref[2 * nblk : 2 * nblk + 8, :] = jnp.broadcast_to(anchor, (8, LANES))


def denom(gathered, counts, ex, offt, extra=()):
    nblk, nk = offt.shape
    rows = jax.ShapeDtypeStruct((nblk, LANES), jnp.float32)
    if extra:
        rows = (
            jax.ShapeDtypeStruct((2 * nblk + 8, LANES), jnp.float32),
            jax.ShapeDtypeStruct((1, nk), jnp.float32),
        )
    return pl.pallas_call(
        last_kernel if extra else denom_kernel,
        out_shape=rows,
        in_specs=[WHOLE] * (3 + PIECES + len(extra)),
        out_specs=(WHOLE, WHOLE) if extra else WHOLE,
        scratch_shapes=[pltpu.VMEM((nblk, nk), jnp.float32), pltpu.VMEM((nblk, LANES), jnp.float32)],
        compiler_params=params(8),
        name="last" if extra else "denom",
    )(gathered, counts, *(pltpu.with_memory_space_constraint(e, VMEM) for e in ex), offt, *extra)


def pair_kernel(a_ref, b_ref, out_ref):
    rows = LANES
    out_ref[0:rows, :] = lse([a_ref[0:rows, :], b_ref[0:rows, :]])
    if out_ref.shape[0] > rows:
        out_ref[rows:, :] = a_ref[rows:, :] + b_ref[rows:, :]


def paired(value, size):
    return pl.pallas_call(
        pair_kernel,
        out_shape=jax.ShapeDtypeStruct(value.shape, value.dtype),
        in_specs=[WHOLE] * 2,
        out_specs=WHOLE,
        compiler_params=params(4),
        name="pair",
    )(value, partner(value, size))


def shift_state(value, size, move):
    return lax.ppermute(value, "state", [(i, move(i)) for i in range(size)])


def partner(value, size):
    return shift_state(value, size, lambda i: i ^ 1)


def others(value, size):
    return [
        shift_state(value, size, lambda i, d=d: (i + 2 * d) % size) for d in range(1, size // 2)
    ]


def shards(samp, state, energies, offsets, counts, labels):
    nk, width = energies.shape
    nblk = offsets.shape[1]
    mine = jnp.broadcast_to(lax.axis_index("state"), (1, 1)).astype(jnp.int32)
    counts_row = counts.reshape(1, nk)
    *ex, offt, sums, local_label, root = prep(
        energies, offsets, counts_row, labels.reshape(nblk, width // nblk), mine
    )
    picked = None
    for step in range(ITERS):
        pair = paired(sums, state)
        parts = [pair, *others(pair, state)]
        if picked is None:
            picked = pick(energies, local_label, pair)
            out = update(parts, ex, offt, samp, (picked,))
        else:
            out = update(parts, ex, offt, samp)
        gathered = lax.all_to_all(out, "samp", 0, 0, tiled=True)
        if step < ITERS - 1:
            sums = denom(gathered, counts_row, ex, offt)
    both, free = denom(gathered, counts_row, ex, offt, (local_label, picked, root))
    pair = paired(both, state)
    parts = [pair, *others(pair, state)]
    d = lse([p[:nblk] for p in parts])
    rest = sum(p[nblk:] for p in parts)
    own = (rest[:nblk] - d).reshape(width)
    return (free - rest[nblk : nblk + 1, 0:1]).reshape(nk), own


def solution(mesh):
    return jax.shard_map(
        functools.partial(shards, mesh.shape["samp"], mesh.shape["state"]),
        mesh=mesh,
        in_specs=(P("state", "samp"), P("state", "samp"), P("state"), P("samp")),
        out_specs=(P("state"), P("samp")),
        check_vma=False,
    )
```

time: 1040 us -> 142 us (0.14)
  waiting for transfers between devices: 421 us -> 22.4 us
  other arithmetic: 273 us -> 1.94 us
  blocking collectives: 216 us -> 32.3 us
  local copies, waits for them, and re-layouts: 63.2 us -> 2.98 us
  Pallas kernels: 0 us -> 58.9 us
  loops' own time: 43.2 us -> 0 us
  starting transfers between devices: 0.51 us -> 21.4 us
  between operations: 14.9 us -> 0.75 us
    psum x4 -> x0, waiting for transfers between devices: 225 us -> none  [the longest x3 174 us: sample_denominator(): total = lax.psum(jnp.sum(jnp.exp(terms - best[None, :]), axis=0), 'state')]
    pmax x4 -> x0, waiting for transfers between devices: 196 us -> none  [sample_denominator(): best = lax.pmax(jnp.max(terms, axis=0), 'state')]
    reduce_sum x39 -> x0, other arithmetic: 150 us -> none  [the longest x4 64.4 us: sample_denominator(): total = lax.psum(jnp.sum(jnp.exp(terms - best[None, :]), axis=0), 'state')]
    reduce_max x7 -> x0, other arithmetic: 116 us -> none  [the longest x4 78 us: sample_denominator(): best = lax.pmax(jnp.max(terms, axis=0), 'state')]
    psum x4 -> x0, blocking collectives: 115 us -> none  [the longest x3 85.7 us: state_update(): total = lax.psum(jnp.sum(jnp.exp(terms - best[:, None]), axis=1), 'samp')]
    pmax x3 -> x0, blocking collectives: 101 us -> none  [state_update(): best = lax.pmax(jnp.max(terms, axis=1), 'samp')]
    pallas_call x0 -> x12, Pallas kernels: none -> 58.9 us  [the longest x1 18.9 us: prep(): pl.pallas_call(prep_kernel, out_shape=(pltpu.VMEM((width // PIECES, nk),...]
    another operation x1 -> x0, loops' own time: 43.2 us -> none  [own_terms_local(): return lax.map(one, jnp.arange(steps_count, dtype=jnp.int32)).reshape(width)]
  transfers between devices with their start and end apart: 8 -> 16, of which waited for: 7 -> 13; matrix products, arithmetic and copies ran while one was open for 9% -> 0% of each run, Pallas kernels for 0% -> 9%
where the time goes in v1:
time: 142 us; the launch traced here: 141 us
  Pallas kernels  58.9 us (41%)
  blocking collectives  32.3 us (23%)
  waiting for transfers between devices  22.4 us (16%)
  starting transfers between devices  21.4 us (15%)
  local copies, waits for them, and re-layouts  2.98 us (2%)
  other arithmetic  1.94 us (1%)
    all_to_all x3, blocking collectives, shards(): gathered = lax.all_to_all(out, 'samp', 0, 0, tiled=True)  32.3 us
    ppermute x16, waiting for transfers between devices, shift_state(): return lax.ppermute(value, 'state', [(i, move(i)) for i in range(size)])  22.4 us
    ppermute x16, starting transfers between devices, shift_state(): return lax.ppermute(value, 'state', [(i, move(i)) for i in range(size)])  21.4 us
    pallas_call x1, Pallas kernels, prep(): pl.pallas_call(prep_kernel, out_shape=(pltpu.VMEM((width // PIECES, nk),...  18.9 us
    pallas_call x3, Pallas kernels, update(): pl.pallas_call(functools.partial(update_kernel, len(parts)), out_shape=ja...  14.9 us
    pallas_call x1, Pallas kernels, pick(): pl.pallas_call(pick_kernel, grid=(width // span,), out_shape=jax.ShapeDty...  12.8 us
    pallas_call x3, Pallas kernels, denom(): pl.pallas_call(last_kernel if extra else denom_kernel, out_shape=rows, in...  12.2 us
  transfers between devices with their start and end apart: 16, of which 13 were waited for; matrix products, arithmetic and copies ran while one was open for 0% of the time, Pallas kernels for 9%

profile of v1, /device:TPU:1, one launch (start us, length us, event | category | flops | bytes accessed | tf_op | source)
XLA Modules:
  0.0 140.7 jit_solution(9788964776419555125)
XLA Ops:
  0.6 0.0 copy-start
  0.6 0.9 copy-done
  1.6 0.0 copy-start.1
  1.6 0.8 copy-done.1
  2.4 0.0 copy-start.2
  2.4 0.7 copy-done.2
  3.1 18.9 %prep.1 = (f32[8192,512]{1,0:T(8,128)S(1)}, f32[8192,512]{1,0:T(8,128)S(1)}, f32[128,512]{1,0:T(8,128)S(1)}, f32[128,128]{1,0:T(8,128)S(1)}, s32[128,128]{1,0:T(8,128)S(1)}, /*index=5*/s32[1,1]{1,0:T(1,128)}) custom-call(bf16[512,16384]{1,0:T(8,128)(2,1)} %e_ref.1, f32[512,128]{1,0:T(8,128)S(1)} %copy-done, s32[1,512]{1,0:T(1,128)S(1)} %bitcast.8, ...), custom_call_target="tpu_custom_call" | custom-call | tf_op jit(solution)/shard_map/prep/pallas_call | solution.py:110
  22.0 1.5 %collective-permute-start = (f32[128,128]{1,0:T(8,128)S(1)}, f32[128,128]{1,0:T(8,128)S(1)}, u32[]{:S(2)}, u32[]{:S(2)}) collective-permute-start(f32[128,128]{1,0:T(8,128)S(1)} %get-tuple-element.10.a_ref), channel_id=1, source_target_pairs={{0,1},{1,0},{2,3},{3,2},{4,5},{5,4},{6,7},{7,6},{8,9},{9,8},{10,11... | collective-permute-start | bytes 196616 | tf_op jit(solution)/shard_map/ppermute | solution.py:310
  23.5 0.9 collective-permute-done.b_ref
  24.4 2.9 %collective-permute-start.3 = (f32[128,128]{1,0:T(8,128)S(1)}, f32[128,128]{1,0:T(8,128)S(1)}, u32[]{:S(2)}, u32[]{:S(2)}) collective-permute-start(f32[128,128]{1,0:T(8,128)S(1)} %pair.4._.refs_0_), channel_id=1, source_target_pairs={{0,6},{1,7},{2,0},{3,1},{4,2},{5,3},{6,4},{7,5},{8,14},{9,15},{10,... | collective-permute-start | bytes 196616 | tf_op jit(solution)/shard_map/ppermute | solution.py:310
  27.3 0.3 collective-permute-start.2
  27.7 0.7 collective-permute-start.1
  28.4 12.8 %pick.1.refs_7_.refs_4_ = f32[128,128]{1,0:T(8,128)S(1)} custom-call(bf16[512,16384]{1,0:T(8,128)(2,1)} %e_ref.1, s32[128,128]{1,0:T(8,128)S(1)} %get-tuple-element.14.label_ref.refs_3_, f32[128,128]{1,0:T(8,128)S(1)} %pair.4._.refs_0_), custom_call_target="tpu_custom_call" | custom-call | flops 25165824 | bytes 16777216 | tf_op jit(solution)/shard_map/pick/pallas_call | solution.py:146
  41.2 0.0 collective-permute-done.3.refs_3_
  41.2 0.0 collective-permute-done.2.refs_2_
  41.2 0.0 collective-permute-done.1.refs_1_
  41.2 5.0 %update.3 = f32[16,1,512]{2,1,0:T(1,128)S(1)} custom-call(f32[128,128]{1,0:T(8,128)S(1)} %pair.4._.refs_0_, f32[128,128]{1,0:T(8,128)S(1)} %collective-permute-done.1.refs_1_, f32[128,128]{1,0:T(8,128)S(1)} %collective-permute-done.2.refs_2_, f32[128,128]{1,0:T(8,128)S(1)} %collective-permute-done.3.refs_3_, ...), custom_call_target="tpu_custom_call" | custom-call | tf_op jit(solution)/shard_map/update/pallas_call | solution.py:206
  46.1 13.8 %all_to_all.15.gathered_ref = f32[16,1,512]{2,1,0:T(1,128)S(1)} all-to-all(f32[16,1,512]{2,1,0:T(1,128)S(1)} %update.3), channel_id=1, replica_groups=mesh['samp'=16,'state'=8] {'samp'}, dimensions={0} | all-to-all | bytes 65536 | tf_op jit(solution)/shard_map/all_to_all | solution.py:340
  60.0 3.8 %denom.2.a_ref = f32[128,128]{1,0:T(8,128)S(1)} custom-call(f32[16,1,512]{2,1,0:T(1,128)S(1)} %all_to_all.15.gathered_ref, s32[1,512]{1,0:T(1,128)S(1)} %bitcast.9, f32[8192,512]{1,0:T(8,128)S(1)} %get-tuple-element.11.refs_4_.refs_0_, f32[8192,512]{1,0:T(8,128)S(1)} %get-tuple-element.12.refs_5_.refs_1_, f32[128,512]{1,0:T(8,128)S(1)} %get-tuple-element.13.refs_6_.refs_2_), custom_call_target="tpu_custom_call" | custom-call | tf_op jit(solution)/shard_map/denom/pallas_call | solution.py:280
  63.8 2.7 %collective-permute-start.4 = (f32[128,128]{1,0:T(8,128)S(1)}, f32[128,128]{1,0:T(8,128)S(1)}, u32[]{:S(2)}, u32[]{:S(2)}) collective-permute-start(f32[128,128]{1,0:T(8,128)S(1)} %denom.2.a_ref), channel_id=1, source_target_pairs={{0,1},{1,0},{2,3},{3,2},{4,5},{5,4},{6,7},{7,6},{8,9},{9,8},{10,11... | collective-permute-start | bytes 196616 | tf_op jit(solution)/shard_map/ppermute | solution.py:310
  66.5 0.9 collective-permute-done.4.b_ref
  67.4 2.1 %collective-permute-start.7 = (f32[128,128]{1,0:T(8,128)S(1)}, f32[128,128]{1,0:T(8,128)S(1)}, u32[]{:S(2)}, u32[]{:S(2)}) collective-permute-start(f32[128,128]{1,0:T(8,128)S(1)} %pair.5.refs_0_), channel_id=1, source_target_pairs={{0,6},{1,7},{2,0},{3,1},{4,2},{5,3},{6,4},{7,5},{8,14},{9,15},{10,... | collective-permute-start | bytes 196616 | tf_op jit(solution)/shard_map/ppermute | solution.py:310
  69.5 1.4 %collective-permute-start.6 = (f32[128,128]{1,0:T(8,128)S(1)}, f32[128,128]{1,0:T(8,128)S(1)}, u32[]{:S(2)}, u32[]{:S(2)}) collective-permute-start(f32[128,128]{1,0:T(8,128)S(1)} %pair.5.refs_0_), channel_id=1, source_target_pairs={{0,4},{1,5},{2,6},{3,7},{4,0},{5,1},{6,2},{7,3},{8,12},{9,13},{10,... | collective-permute-start | bytes 196616 | tf_op jit(solution)/shard_map/ppermute | solution.py:310
  70.9 0.0 collective-permute-start.5
  70.9 0.2 collective-permute-done.7.refs_3_
  71.2 3.0 %collective-permute-done.6.refs_2_ = f32[128,128]{1,0:T(8,128)S(1)} collective-permute-done((f32[128,128]{1,0:T(8,128)S(1)}, f32[128,128]{1,0:T(8,128)S(1)}, u32[]{:S(2)}, u32[]{:S(2)}) %collective-permute-start.6) | collective-permute-done | bytes 65568 | tf_op jit(solution)/shard_map/ppermute | solution.py:310
  74.1 1.8 %collective-permute-done.5.refs_1_ = f32[128,128]{1,0:T(8,128)S(1)} collective-permute-done((f32[128,128]{1,0:T(8,128)S(1)}, f32[128,128]{1,0:T(8,128)S(1)}, u32[]{:S(2)}, u32[]{:S(2)}) %collective-permute-start.5) | collective-permute-done | bytes 65568 | tf_op jit(solution)/shard_map/ppermute | solution.py:310
  75.9 5.0 %update.4 = f32[16,1,512]{2,1,0:T(1,128)S(1)} custom-call(f32[128,128]{1,0:T(8,128)S(1)} %pair.5.refs_0_, f32[128,128]{1,0:T(8,128)S(1)} %collective-permute-done.5.refs_1_, f32[128,128]{1,0:T(8,128)S(1)} %collective-permute-done.6.refs_2_, f32[128,128]{1,0:T(8,128)S(1)} %collective-permute-done.7.refs_3_, ...), custom_call_target="tpu_custom_call" | custom-call | tf_op jit(solution)/shard_map/update/pallas_call | solution.py:206
  80.9 9.2 %all_to_all.16.gathered_ref = f32[16,1,512]{2,1,0:T(1,128)S(1)} all-to-all(f32[16,1,512]{2,1,0:T(1,128)S(1)} %update.4), channel_id=1, replica_groups=mesh['samp'=16,'state'=8] {'samp'}, dimensions={0} | all-to-all | bytes 65536 | tf_op jit(solution)/shard_map/all_to_all | solution.py:340
  90.1 3.8 %denom.3.a_ref = f32[128,128]{1,0:T(8,128)S(1)} custom-call(f32[16,1,512]{2,1,0:T(1,128)S(1)} %all_to_all.16.gathered_ref, s32[1,512]{1,0:T(1,128)S(1)} %bitcast.10, f32[8192,512]{1,0:T(8,128)S(1)} %get-tuple-element.11.refs_4_.refs_0_, f32[8192,512]{1,0:T(8,128)S(1)} %get-tuple-element.12.refs_5_.refs_1_, f32[128,512]{1,0:T(8,128)S(1)} %get-tuple-element.13.refs_6_.refs_2_), custom_call_target="tpu_custom_call" | custom-call | tf_op jit(solution)/shard_map/denom/pallas_call | solution.py:280
  93.9 2.9 %collective-permute-start.8 = (f32[128,128]{1,0:T(8,128)S(1)}, f32[128,128]{1,0:T(8,128)S(1)}, u32[]{:S(2)}, u32[]{:S(2)}) collective-permute-start(f32[128,128]{1,0:T(8,128)S(1)} %denom.3.a_ref), channel_id=1, source_target_pairs={{0,1},{1,0},{2,3},{3,2},{4,5},{5,4},{6,7},{7,6},{8,9},{9,8},{10,11... | collective-permute-start | bytes 196616 | tf_op jit(solution)/shard_map/ppermute | solution.py:310
  96.8 0.9 collective-permute-done.8.b_ref
  97.8 0.1 collective-permute-start.11
  97.9 1.3 collective-permute-start.10
  99.1 0.6 collective-permute-start.9
  99.7 1.3 collective-permute-done.11.refs_3_
  101.0 1.6 %collective-permute-done.10.refs_2_ = f32[128,128]{1,0:T(8,128)S(1)} collective-permute-done((f32[128,128]{1,0:T(8,128)S(1)}, f32[128,128]{1,0:T(8,128)S(1)}, u32[]{:S(2)}, u32[]{:S(2)}) %collective-permute-start.10) | collective-permute-done | bytes 65568 | tf_op jit(solution)/shard_map/ppermute | solution.py:310
  102.6 1.6 %collective-permute-done.9.refs_1_ = f32[128,128]{1,0:T(8,128)S(1)} collective-permute-done((f32[128,128]{1,0:T(8,128)S(1)}, f32[128,128]{1,0:T(8,128)S(1)}, u32[]{:S(2)}, u32[]{:S(2)}) %collective-permute-start.9) | collective-permute-done | bytes 65568 | tf_op jit(solution)/shard_map/ppermute | solution.py:310
  104.1 5.0 %update.5 = f32[16,1,512]{2,1,0:T(1,128)S(1)} custom-call(f32[128,128]{1,0:T(8,128)S(1)} %pair.6.refs_0_, f32[128,128]{1,0:T(8,128)S(1)} %collective-permute-done.9.refs_1_, f32[128,128]{1,0:T(8,128)S(1)} %collective-permute-done.10.refs_2_, f32[128,128]{1,0:T(8,128)S(1)} %collective-permute-done.11.refs_3_, ...), custom_call_target="tpu_custom_call" | custom-call | tf_op jit(solution)/shard_map/update/pallas_call | solution.py:206
  109.1 9.2 %all_to_all.17.gathered_ref = f32[16,1,512]{2,1,0:T(1,128)S(1)} all-to-all(f32[16,1,512]{2,1,0:T(1,128)S(1)} %update.5), channel_id=1, replica_groups=mesh['samp'=16,'state'=8] {'samp'}, dimensions={0} | all-to-all | bytes 65536 | tf_op jit(solution)/shard_map/all_to_all | solution.py:340
  118.3 4.6 %last.1 = (f32[264,128]{1,0:T(8,128)S(1)}, f32[1,512]{1,0:T(1,128)S(1)}) custom-call(f32[16,1,512]{2,1,0:T(1,128)S(1)} %all_to_all.17.gathered_ref, s32[1,512]{1,0:T(1,128)S(1)} %bitcast.11, f32[8192,512]{1,0:T(8,128)S(1)} %get-tuple-element.11.refs_4_.refs_0_, f32[8192,512]{1,0:T(8,128)S(1)} %get-tuple-element.12.refs_5_.refs_1_, ...), custom_call_target="tpu_custom_call" | custom-call | tf_op jit(solution)/shard_map/last/pallas_call | solution.py:280
  122.9 2.9 %collective-permute-start.12 = (f32[264,128]{1,0:T(8,128)S(1)}, f32[264,128]{1,0:T(8,128)S(1)}, u32[]{:S(2)}, u32[]{:S(2)}) collective-permute-start(f32[264,128]{1,0:T(8,128)S(1)} %get-tuple-element.17.a_ref), channel_id=1, source_target_pairs={{0,1},{1,0},{2,3},{3,2},{4,5},{5,4},{6,7},{7,6},{8,9},{9,8},{10,11... | collective-permute-start | bytes 405512 | tf_op jit(solution)/shard_map/ppermute | solution.py:310
  125.8 1.0 collective-permute-done.12.b_ref
  126.9 1.4 %collective-permute-start.15 = (f32[264,128]{1,0:T(8,128)S(1)}, f32[264,128]{1,0:T(8,128)S(1)}, u32[]{:S(2)}, u32[]{:S(2)}) collective-permute-start(f32[264,128]{1,0:T(8,128)S(1)} %pair.7), channel_id=1, source_target_pairs={{0,6},{1,7},{2,0},{3,1},{4,2},{5,3},{6,4},{7,5},{8,14},{9,15},{10,... | collective-permute-start | bytes 405512 | tf_op jit(solution)/shard_map/ppermute | solution.py:310
  128.3 0.6 collective-permute-start.14
  128.9 0.0 collective-permute-start.13
  129.0 2.8 %collective-permute-done.15 = f32[264,128]{1,0:T(8,128)S(1)} collective-permute-done((f32[264,128]{1,0:T(8,128)S(1)}, f32[264,128]{1,0:T(8,128)S(1)}, u32[]{:S(2)}, u32[]{:S(2)}) %collective-permute-start.15) | collective-permute-done | bytes 135200 | tf_op jit(solution)/shard_map/ppermute | solution.py:310
  131.7 2.5 %collective-permute-done.14 = f32[264,128]{1,0:T(8,128)S(1)} collective-permute-done((f32[264,128]{1,0:T(8,128)S(1)}, f32[264,128]{1,0:T(8,128)S(1)}, u32[]{:S(2)}, u32[]{:S(2)}) %collective-permute-start.14) | collective-permute-done | bytes 135200 | tf_op jit(solution)/shard_map/ppermute | solution.py:310
  134.3 3.9 %collective-permute-done.13 = f32[264,128]{1,0:T(8,128)S(1)} collective-permute-done((f32[264,128]{1,0:T(8,128)S(1)}, f32[264,128]{1,0:T(8,128)S(1)}, u32[]{:S(2)}, u32[]{:S(2)}) %collective-permute-start.13) | collective-permute-done | bytes 135200 | tf_op jit(solution)/shard_map/ppermute | solution.py:310
  138.2 0.5 slice.44
  138.7 1.2 broadcast_subtract_fusion
  140.0 0.7 fusion
  (5 shorter events, 0.2 us)
Async XLA Ops:
  0.6 1.0 copy-start
  1.6 0.8 copy-start.1
  2.4 0.7 copy-start.2
  22.0 2.4 %collective-permute-start = (f32[128,128]{1,0:T(8,128)S(1)}, f32[128,128]{1,0:T(8,128)S(1)}, u32[]{:S(2)}, u32[]{:S(2)}) collective-permute-start(f32[128,128]{1,0:T(8,128)S(1)} %get-tuple-element.10.a_ref), channel_id=1, source_target_pairs={{0,1},{1,0},{2,3},{3,2},{4,5},{5,4},{6,7},{7,6},{8,9},{9,8},{10,11... | collective-permute-start | bytes 196616 | tf_op jit(solution)/shard_map/ppermute | solution.py:310
  24.4 16.7 %collective-permute-start.3 = (f32[128,128]{1,0:T(8,128)S(1)}, f32[128,128]{1,0:T(8,128)S(1)}, u32[]{:S(2)}, u32[]{:S(2)}) collective-permute-start(f32[128,128]{1,0:T(8,128)S(1)} %pair.4._.refs_0_), channel_id=1, source_target_pairs={{0,6},{1,7},{2,0},{3,1},{4,2},{5,3},{6,4},{7,5},{8,14},{9,15},{10,... | collective-permute-start | bytes 196616 | tf_op jit(solution)/shard_map/ppermute | solution.py:310
  27.3 13.8 %collective-permute-start.2 = (f32[128,128]{1,0:T(8,128)S(1)}, f32[128,128]{1,0:T(8,128)S(1)}, u32[]{:S(2)}, u32[]{:S(2)}) collective-permute-start(f32[128,128]{1,0:T(8,128)S(1)} %pair.4._.refs_0_), channel_id=1, source_target_pairs={{0,4},{1,5},{2,6},{3,7},{4,0},{5,1},{6,2},{7,3},{8,12},{9,13},{10,... | collective-permute-start | bytes 196616 | tf_op jit(solution)/shard_map/ppermute | solution.py:310
  27.7 13.5 %collective-permute-start.1 = (f32[128,128]{1,0:T(8,128)S(1)}, f32[128,128]{1,0:T(8,128)S(1)}, u32[]{:S(2)}, u32[]{:S(2)}) collective-permute-start(f32[128,128]{1,0:T(8,128)S(1)} %pair.4._.refs_0_), channel_id=1, source_target_pairs={{0,2},{1,3},{2,4},{3,5},{4,6},{5,7},{6,0},{7,1},{8,10},{9,11},{10,... | collective-permute-start | bytes 196616 | tf_op jit(solution)/shard_map/ppermute | solution.py:310
  63.8 3.6 %collective-permute-start.4 = (f32[128,128]{1,0:T(8,128)S(1)}, f32[128,128]{1,0:T(8,128)S(1)}, u32[]{:S(2)}, u32[]{:S(2)}) collective-permute-start(f32[128,128]{1,0:T(8,128)S(1)} %denom.2.a_ref), channel_id=1, source_target_pairs={{0,1},{1,0},{2,3},{3,2},{4,5},{5,4},{6,7},{7,6},{8,9},{9,8},{10,11... | collective-permute-start | bytes 196616 | tf_op jit(solution)/shard_map/ppermute | solution.py:310
  67.4 3.7 %collective-permute-start.7 = (f32[128,128]{1,0:T(8,128)S(1)}, f32[128,128]{1,0:T(8,128)S(1)}, u32[]{:S(2)}, u32[]{:S(2)}) collective-permute-start(f32[128,128]{1,0:T(8,128)S(1)} %pair.5.refs_0_), channel_id=1, source_target_pairs={{0,6},{1,7},{2,0},{3,1},{4,2},{5,3},{6,4},{7,5},{8,14},{9,15},{10,... | collective-permute-start | bytes 196616 | tf_op jit(solution)/shard_map/ppermute | solution.py:310
  69.5 4.6 %collective-permute-start.6 = (f32[128,128]{1,0:T(8,128)S(1)}, f32[128,128]{1,0:T(8,128)S(1)}, u32[]{:S(2)}, u32[]{:S(2)}) collective-permute-start(f32[128,128]{1,0:T(8,128)S(1)} %pair.5.refs_0_), channel_id=1, source_target_pairs={{0,4},{1,5},{2,6},{3,7},{4,0},{5,1},{6,2},{7,3},{8,12},{9,13},{10,... | collective-permute-start | bytes 196616 | tf_op jit(solution)/shard_map/ppermute | solution.py:310
  70.9 5.0 %collective-permute-start.5 = (f32[128,128]{1,0:T(8,128)S(1)}, f32[128,128]{1,0:T(8,128)S(1)}, u32[]{:S(2)}, u32[]{:S(2)}) collective-permute-start(f32[128,128]{1,0:T(8,128)S(1)} %pair.5.refs_0_), channel_id=1, source_target_pairs={{0,2},{1,3},{2,4},{3,5},{4,6},{5,7},{6,0},{7,1},{8,10},{9,11},{10,... | collective-permute-start | bytes 196616 | tf_op jit(solution)/shard_map/ppermute | solution.py:310
  93.9 3.8 %collective-permute-start.8 = (f32[128,128]{1,0:T(8,128)S(1)}, f32[128,128]{1,0:T(8,128)S(1)}, u32[]{:S(2)}, u32[]{:S(2)}) collective-permute-start(f32[128,128]{1,0:T(8,128)S(1)} %denom.3.a_ref), channel_id=1, source_target_pairs={{0,1},{1,0},{2,3},{3,2},{4,5},{5,4},{6,7},{7,6},{8,9},{9,8},{10,11... | collective-permute-start | bytes 196616 | tf_op jit(solution)/shard_map/ppermute | solution.py:310
  97.8 3.2 %collective-permute-start.11 = (f32[128,128]{1,0:T(8,128)S(1)}, f32[128,128]{1,0:T(8,128)S(1)}, u32[]{:S(2)}, u32[]{:S(2)}) collective-permute-start(f32[128,128]{1,0:T(8,128)S(1)} %pair.6.refs_0_), channel_id=1, source_target_pairs={{0,6},{1,7},{2,0},{3,1},{4,2},{5,3},{6,4},{7,5},{8,14},{9,15},{10,... | collective-permute-start | bytes 196616 | tf_op jit(solution)/shard_map/ppermute | solution.py:310
  97.9 4.7 %collective-permute-start.10 = (f32[128,128]{1,0:T(8,128)S(1)}, f32[128,128]{1,0:T(8,128)S(1)}, u32[]{:S(2)}, u32[]{:S(2)}) collective-permute-start(f32[128,128]{1,0:T(8,128)S(1)} %pair.6.refs_0_), channel_id=1, source_target_pairs={{0,4},{1,5},{2,6},{3,7},{4,0},{5,1},{6,2},{7,3},{8,12},{9,13},{10,... | collective-permute-start | bytes 196616 | tf_op jit(solution)/shard_map/ppermute | solution.py:310
  99.1 5.0 %collective-permute-start.9 = (f32[128,128]{1,0:T(8,128)S(1)}, f32[128,128]{1,0:T(8,128)S(1)}, u32[]{:S(2)}, u32[]{:S(2)}) collective-permute-start(f32[128,128]{1,0:T(8,128)S(1)} %pair.6.refs_0_), channel_id=1, source_target_pairs={{0,2},{1,3},{2,4},{3,5},{4,6},{5,7},{6,0},{7,1},{8,10},{9,11},{10,... | collective-permute-start | bytes 196616 | tf_op jit(solution)/shard_map/ppermute | solution.py:310
  122.9 3.9 %collective-permute-start.12 = (f32[264,128]{1,0:T(8,128)S(1)}, f32[264,128]{1,0:T(8,128)S(1)}, u32[]{:S(2)}, u32[]{:S(2)}) collective-permute-start(f32[264,128]{1,0:T(8,128)S(1)} %get-tuple-element.17.a_ref), channel_id=1, source_target_pairs={{0,1},{1,0},{2,3},{3,2},{4,5},{5,4},{6,7},{7,6},{8,9},{9,8},{10,11... | collective-permute-start | bytes 405512 | tf_op jit(solution)/shard_map/ppermute | solution.py:310
  126.9 4.9 %collective-permute-start.15 = (f32[264,128]{1,0:T(8,128)S(1)}, f32[264,128]{1,0:T(8,128)S(1)}, u32[]{:S(2)}, u32[]{:S(2)}) collective-permute-start(f32[264,128]{1,0:T(8,128)S(1)} %pair.7), channel_id=1, source_target_pairs={{0,6},{1,7},{2,0},{3,1},{4,2},{5,3},{6,4},{7,5},{8,14},{9,15},{10,... | collective-permute-start | bytes 405512 | tf_op jit(solution)/shard_map/ppermute | solution.py:310
  128.3 6.0 %collective-permute-start.14 = (f32[264,128]{1,0:T(8,128)S(1)}, f32[264,128]{1,0:T(8,128)S(1)}, u32[]{:S(2)}, u32[]{:S(2)}) collective-permute-start(f32[264,128]{1,0:T(8,128)S(1)} %pair.7), channel_id=1, source_target_pairs={{0,4},{1,5},{2,6},{3,7},{4,0},{5,1},{6,2},{7,3},{8,12},{9,13},{10,... | collective-permute-start | bytes 405512 | tf_op jit(solution)/shard_map/ppermute | solution.py:310
  128.9 9.3 %collective-permute-start.13 = (f32[264,128]{1,0:T(8,128)S(1)}, f32[264,128]{1,0:T(8,128)S(1)}, u32[]{:S(2)}, u32[]{:S(2)}) collective-permute-start(f32[264,128]{1,0:T(8,128)S(1)} %pair.7), channel_id=1, source_target_pairs={{0,2},{1,3},{2,4},{3,5},{4,6},{5,7},{6,0},{7,1},{8,10},{9,11},{10,... | collective-permute-start | bytes 405512 | tf_op jit(solution)/shard_map/ppermute | solution.py:310

commit v2 on v1

v2 whole, which is shorter than its diff:
```python
import functools

import jax
import jax.numpy as jnp
from jax import lax
from jax.experimental import pallas as pl
from jax.experimental.pallas import tpu as pltpu
from jax.sharding import PartitionSpec as P

ITERS = 3
LANES = 128
GROUP = 8
PIECES = 2
UNROLL_UPDATE = 1
UNROLL_DENOM = 8
VMEM = pltpu.VMEM
WHOLE = pl.BlockSpec(memory_space=pltpu.VMEM)


def params(mib):
    return pltpu.CompilerParams(vmem_limit_bytes=mib << 20)


def block_weights(lead, offt_ref, w_ref, top_ref):
    h = lead - offt_ref[...]
    top = jnp.max(h, axis=1, keepdims=True)
    top_ref[...] = jnp.broadcast_to(top, top_ref.shape)
    w_ref[...] = jnp.exp(h - top)


def spread(ref, g, j, q):
    tile = ref[pl.ds(pl.multiple_of(g * GROUP, GROUP), GROUP), q * LANES : (q + 1) * LANES]
    return jnp.broadcast_to(tile[j : j + 1, :], (8, LANES))


def row_sums(load, w_ref, g, j, acc, rows):
    lane = lax.broadcasted_iota(jnp.int32, (8, acc[0].shape[1]), 1)
    here = lane == g * GROUP + j
    nq = w_ref.shape[1] // LANES
    w = [spread(w_ref, g, j, q) for q in range(nq)]
    out = []
    for i in range(rows // 8):
        total = load(i, 0) * w[0]
        for q in range(1, nq):
            total = total + load(i, q) * w[q]
        col = jnp.sum(total, axis=1, keepdims=True)
        out.append(jnp.where(here, col, acc[i]))
    return tuple(out)


def log_rows(acc, top_ref):
    return top_ref[...] + jnp.log(jnp.concatenate(acc, axis=0).T)


def over_pieces(step, ex_refs, steps, carry, unroll=1):
    each = steps // len(ex_refs)
    for p, ex_ref in enumerate(ex_refs):
        carry = lax.fori_loop(p * each, (p + 1) * each, functools.partial(step, ex_ref, p * each), carry, unroll=unroll)
    return carry


def prep_kernel(e_hbm, off_hbm, counts_hbm, labels_hbm, mine_ref, *refs):
    ex_refs, outs = refs[:PIECES], refs[PIECES:]
    offt_ref, out_ref, local_ref, who_ref, counts_ref, buf, sem, off_ref, small_sem, w_ref, top_ref = outs
    nk, span = buf.shape[1:]
    depth = buf.shape[0]
    steps = e_hbm.shape[1] // span
    side = 2 * LANES
    nq = nk // LANES

    def copy(step, slot):
        at = pl.multiple_of(step * span, span)
        return pltpu.make_async_copy(e_hbm.at[:, pl.ds(at, span)], buf.at[slot], sem.at[slot])

    small = [
        pltpu.make_async_copy(src, dst, small_sem.at[n])
        for n, (src, dst) in enumerate(
            [(off_hbm, off_ref), (counts_hbm, counts_ref), (labels_hbm, local_ref)]
        )
    ]
    for c in small:
        c.start()
    for n in range(depth - 1):
        copy(n, n).start()
    eye = lax.broadcasted_iota(jnp.int32, (side, side), 0) == lax.broadcasted_iota(jnp.int32, (side, side), 1)
    minus = jnp.where(eye, -1.0, 0.0).astype(jnp.bfloat16)
    for c in small:
        c.wait()
    mine = mine_ref[...]
    local_ref[...] = local_ref[...] - mine * nk
    who_ref[...] = mine
    offt_ref[...] = off_ref[...].T
    block_weights(jnp.log(counts_ref[...].astype(jnp.float32)), offt_ref, w_ref, top_ref)

    def step(ex_ref, first, g, acc):
        slot = lax.rem(g, depth)

        @pl.when(g + depth - 1 < steps)
        def _():
            copy(g + depth - 1, lax.rem(g + depth - 1, depth)).start()

        copy(g, slot).wait()
        for c in range(span // side):
            base = pl.multiple_of((g - first) * span + c * side, side)
            pieces = []
            for q in range(nk // side):
                tile = buf[slot, q * side : (q + 1) * side, c * side : (c + 1) * side]
                turned = lax.dot_general(
                    minus, tile, (((1,), (1,)), ((), ())), preferred_element_type=jnp.float32
                )
                value = jnp.exp(turned)
                ex_ref[pl.ds(base, side), q * side : (q + 1) * side] = value
                pieces.append(value)

            for half in range(2):

                def load(i, q, half=half):
                    at = half * LANES + i * 8
                    lane = (q % 2) * LANES
                    return pieces[q // 2][at : at + 8, lane : lane + LANES]

                acc = row_sums(load, w_ref, g, 2 * c + half, acc, LANES)
        return acc

    acc = (jnp.zeros((8, out_ref.shape[0]), jnp.float32),) * (LANES // 8)
    acc = over_pieces(step, ex_refs, steps, acc)
    out_ref[...] = log_rows(acc, top_ref)


def prep(energies, offsets, counts, labels, mine):
    nk, width = energies.shape
    nblk = offsets.shape[1]
    span = GROUP * LANES
    depth = 4
    anywhere = pl.BlockSpec(memory_space=pl.ANY)
    return pl.pallas_call(
        prep_kernel,
        out_shape=(pltpu.VMEM((width // PIECES, nk), jnp.float32),) * PIECES + (
            jax.ShapeDtypeStruct((nblk, nk), jnp.float32),
            jax.ShapeDtypeStruct((nblk, LANES), jnp.float32),
            jax.ShapeDtypeStruct(labels.shape, jnp.int32),
            jax.ShapeDtypeStruct((1, 1), jnp.int32),
            jax.ShapeDtypeStruct((1, nk), jnp.int32),
        ),
        in_specs=[anywhere] * 4 + [WHOLE],
        out_specs=(WHOLE,) * (PIECES + 5),
        scratch_shapes=[
            pltpu.VMEM((depth, nk, span), jnp.bfloat16),
            pltpu.SemaphoreType.DMA((depth,)),
            pltpu.VMEM((nk, nblk), jnp.float32),
            pltpu.SemaphoreType.DMA((3,)),
            pltpu.VMEM((nblk, nk), jnp.float32),
            pltpu.VMEM((nblk, LANES), jnp.float32),
        ],
        compiler_params=params(12),
        name="prep",
    )(*(pltpu.with_memory_space_constraint(a, pltpu.HBM) for a in (energies, offsets, counts, labels)), mine)


def pick_kernel(e_ref, label_ref, _, out_ref):
    nk, span = e_ref.shape
    kid = lax.broadcasted_iota(jnp.int32, (16, LANES), 0).astype(jnp.int16)
    far = jnp.int32(-1)
    for j in range(span // LANES):
        label = label_ref[j : j + 1, :]
        label = jnp.where((label >= 0) & (label < nk), label, far)
        want = jnp.broadcast_to(label, (16, LANES)).astype(jnp.int16)
        acc = [jnp.zeros((16, LANES), jnp.bfloat16) for _ in range(2)]
        for k in range(nk // 16):
            tile = e_ref[k * 16 : (k + 1) * 16, j * LANES : (j + 1) * LANES]
            acc[k % 2] = jnp.where(want == kid + jnp.int16(k * 16), tile, acc[k % 2])
        both = acc[0].astype(jnp.float32) + acc[1].astype(jnp.float32)
        out_ref[j : j + 1, :] = jnp.sum(both, axis=0, keepdims=True)


def pick(energies, local_label, first, count, after):
    nk = energies.shape[0]
    span = GROUP * LANES
    return pl.pallas_call(
        pick_kernel,
        grid=(count,),
        out_shape=jax.ShapeDtypeStruct((count * GROUP, LANES), jnp.float32),
        in_specs=[
            pl.BlockSpec((nk, span), lambda i: (0, i + first)),
            pl.BlockSpec((GROUP, LANES), lambda i: (i + first, 0)),
            pl.BlockSpec(memory_space=pl.ANY),
        ],
        out_specs=pl.BlockSpec((GROUP, LANES), lambda i: (i, 0)),
        compiler_params=params(8),
        cost_estimate=pl.CostEstimate(
            flops=count * span * nk * 3, bytes_accessed=count * span * nk * 2, transcendentals=0
        ),
        name="pick",
    )(pltpu.with_memory_space_constraint(energies, pltpu.HBM), local_label, after)


def lse(values):
    best = functools.reduce(jnp.maximum, values)
    return best + jnp.log(sum(jnp.exp(v - best) for v in values))


def update_kernel(n_in, *refs):
    parts, ex_refs, offt_ref = refs[:n_in], refs[n_in : n_in + PIECES], refs[n_in + PIECES]
    out_ref, vt_ref, g_ref = refs[-3:]
    nblk, nk = offt_ref.shape
    nq = nk // LANES
    d = lse([p[...] for p in parts])
    low = jnp.min(d, axis=1, keepdims=True)
    turned = jnp.exp(low - d).T
    for g in range(nblk // GROUP):
        vt_ref[g * LANES : (g + 1) * LANES, :] = pltpu.roll(turned, (nblk - g * GROUP) % nblk, 1)
    h = -offt_ref[...] - low
    top = jnp.max(h, axis=0, keepdims=True)
    g_ref[...] = jnp.exp(h - top)

    def step(ex_ref, first, g, total):
        for j in range(GROUP):
            acc = [None] * nq
            for i in range(LANES // 8):
                col = vt_ref[pl.ds(pl.multiple_of(g * LANES + i * 8, 8), 8), :]
                v = jnp.broadcast_to(col[:, j : j + 1], (8, LANES))
                at = pl.multiple_of(((g - first) * GROUP + j) * LANES + i * 8, 8)
                for q in range(nq):
                    term = ex_ref[pl.ds(at, 8), q * LANES : (q + 1) * LANES] * v
                    acc[q] = term if acc[q] is None else acc[q] + term
            total = tuple(
                total[q] + acc[q] * spread(g_ref, g, j, q)
                for q in range(nq)
            )
        return total

    zero = jnp.zeros((8, LANES), jnp.float32)
    total = over_pieces(step, ex_refs, nblk // GROUP, (zero,) * nq, UNROLL_UPDATE)
    sums = jnp.concatenate([jnp.sum(t, axis=0, keepdims=True) for t in total], axis=1)
    out_ref[...] = jnp.broadcast_to((top + jnp.log(sums))[None], out_ref.shape)


def update(parts, ex, offt, copies, after=()):
    nblk, nk = offt.shape
    return pl.pallas_call(
        functools.partial(update_kernel, len(parts)),
        out_shape=jax.ShapeDtypeStruct((copies, 1, nk), jnp.float32),
        in_specs=[WHOLE] * (len(parts) + PIECES + 1) + [pl.BlockSpec(memory_space=pl.ANY)] * len(after),
        out_specs=WHOLE,
        scratch_shapes=[
            pltpu.VMEM((nblk // GROUP * LANES, nblk), jnp.float32),
            pltpu.VMEM((nblk, nk), jnp.float32),
        ],
        compiler_params=params(8),
        name="update",
    )(*parts, *(pltpu.with_memory_space_constraint(e, VMEM) for e in ex), offt, *after)


def denom_sums(free, counts_ref, ex_refs, offt_ref, w_ref, top_ref):
    nblk = offt_ref.shape[0]
    lead = jnp.log(counts_ref[...].astype(jnp.float32)) + free
    block_weights(lead, offt_ref, w_ref, top_ref)

    def step(ex_ref, first, g, acc):
        for j in range(GROUP):

            def load(i, q, j=j):
                at = pl.multiple_of(((g - first) * GROUP + j) * LANES + i * 8, 8)
                return ex_ref[pl.ds(at, 8), q * LANES : (q + 1) * LANES]

            acc = row_sums(load, w_ref, g, j, acc, LANES)
        return acc

    acc = (jnp.zeros((8, nblk), jnp.float32),) * (LANES // 8)
    acc = over_pieces(step, ex_refs, nblk // GROUP, acc, UNROLL_DENOM)
    return lead, log_rows(acc, top_ref)


def free_of(gathered):
    best = jnp.max(gathered, axis=0, keepdims=True)
    total = jnp.sum(jnp.exp(gathered - best), axis=0, keepdims=True)
    return -(best + jnp.log(total))[0]


def denom_kernel(gathered_ref, counts_ref, *refs):
    ex_refs, (offt_ref, out_ref, w_ref, top_ref) = refs[:PIECES], refs[PIECES:]
    free = free_of(gathered_ref[...])
    out_ref[...] = denom_sums(free, counts_ref, ex_refs, offt_ref, w_ref, top_ref)[1]


def last_kernel(gathered_ref, counts_ref, *refs):
    ex_refs, (offt_ref, label_ref, who_ref, *refs) = refs[:PIECES], refs[PIECES:]
    *picked_refs, keep_ref, send_ref, free_ref, w_ref, top_ref = refs
    picked = [ref[r * 8 : (r + 1) * 8, :] for ref in picked_refs for r in range(ref.shape[0] // 8)]
    nblk, nk = offt_ref.shape
    half = nblk // 2
    free = free_of(gathered_ref[...])
    free_ref[...] = free
    lead, sums = denom_sums(free, counts_ref, ex_refs, offt_ref, w_ref, top_ref)
    even = (who_ref[...] & 1) == 0
    keep_ref[0:half, :] = jnp.where(even, sums[:half], sums[half:])
    send_ref[0:half, :] = jnp.where(even, sums[half:], sums[:half])
    own = []
    for r in range(nblk // 8):
        at = slice(r * 8, (r + 1) * 8)
        label = label_ref[at, :]
        low = label & (LANES - 1)
        high = label >> 7
        term = jnp.zeros((8, LANES), jnp.float32)
        for q in range(nk // LANES):
            cut = slice(q * LANES, (q + 1) * LANES)
            table = lead[:, cut] - offt_ref[at, cut]
            value = jnp.take_along_axis(table, low, axis=1, mode="promise_in_bounds")
            term = jnp.where(high == q, value - picked[r], term)
        own.append(term)
    for r in range(half // 8):
        first, second = own[r], own[r + half // 8]
        at = slice(half + r * 8, half + (r + 1) * 8)
        keep_ref[at, :] = jnp.where(even, first, second)
        send_ref[at, :] = jnp.where(even, second, first)
    anchor = jnp.broadcast_to(jnp.where(who_ref[...] == 0, free[0:1, 0:1], 0.0), (8, LANES))
    keep_ref[nblk:, :] = anchor
    send_ref[nblk:, :] = anchor


def denom(gathered, counts, ex, offt, extra=()):
    nblk, nk = offt.shape
    rows = jax.ShapeDtypeStruct((nblk, LANES), jnp.float32)
    if extra:
        rows = (
            jax.ShapeDtypeStruct((nblk + 8, LANES), jnp.float32),
            jax.ShapeDtypeStruct((nblk + 8, LANES), jnp.float32),
            jax.ShapeDtypeStruct((1, nk), jnp.float32),
        )
    return pl.pallas_call(
        last_kernel if extra else denom_kernel,
        out_shape=rows,
        in_specs=[WHOLE] * (3 + PIECES + len(extra)),
        out_specs=(WHOLE,) * 3 if extra else WHOLE,
        scratch_shapes=[pltpu.VMEM((nblk, nk), jnp.float32), pltpu.VMEM((nblk, LANES), jnp.float32)],
        compiler_params=params(8),
        name="last" if extra else "denom",
    )(gathered, counts, *(pltpu.with_memory_space_constraint(e, VMEM) for e in ex), offt, *extra)


def pair_kernel(rows, a_ref, b_ref, out_ref):
    out_ref[0:rows, :] = lse([a_ref[0:rows, :], b_ref[0:rows, :]])
    if out_ref.shape[0] > rows:
        out_ref[rows:, :] = a_ref[rows:, :] + b_ref[rows:, :]


def paired(mine, theirs, rows):
    return pl.pallas_call(
        functools.partial(pair_kernel, rows),
        out_shape=jax.ShapeDtypeStruct(mine.shape, mine.dtype),
        in_specs=[WHOLE] * 2,
        out_specs=WHOLE,
        compiler_params=params(4),
        name="pair",
    )(mine, theirs)


def finish_kernel(*refs):
    *parts, free_in, own_ref, free_ref = refs
    half = own_ref.shape[0]
    d = lse([p[0:half, :] for p in parts])
    own_ref[...] = sum(p[half : 2 * half, :] for p in parts) - d
    free_ref[...] = free_in[...] - sum(p[2 * half : 2 * half + 1, 0:1] for p in parts)


def finish(parts, free):
    half = (parts[0].shape[0] - 8) // 2
    return pl.pallas_call(
        finish_kernel,
        out_shape=(jax.ShapeDtypeStruct((half, LANES), jnp.float32), jax.ShapeDtypeStruct(free.shape, jnp.float32)),
        in_specs=[WHOLE] * (len(parts) + 1),
        out_specs=(WHOLE, WHOLE),
        compiler_params=params(4),
        name="finish",
    )(*parts, free)


def join_kernel(mine_ref, theirs_ref, who_ref, out_ref):
    half = mine_ref.shape[0]
    even = (who_ref[...] & 1) == 0
    mine, theirs = mine_ref[...], theirs_ref[...]
    out_ref[0:half, :] = jnp.where(even, mine, theirs)
    out_ref[half:, :] = jnp.where(even, theirs, mine)


def join(mine, theirs, who):
    return pl.pallas_call(
        join_kernel,
        out_shape=jax.ShapeDtypeStruct((2 * mine.shape[0], LANES), jnp.float32),
        in_specs=[WHOLE] * 3,
        out_specs=WHOLE,
        compiler_params=params(4),
        name="join",
    )(mine, theirs, who)


def shift_state(value, size, move):
    return lax.ppermute(value, "state", [(i, move(i)) for i in range(size)])


def partner(value, size):
    return shift_state(value, size, lambda i: i ^ 1)


def others(value, size):
    return [
        shift_state(value, size, lambda i, d=d: (i + 2 * d) % size) for d in range(1, size // 2)
    ]


def shards(samp, state, energies, offsets, counts, labels):
    nk, width = energies.shape
    nblk = offsets.shape[1]
    mine = jnp.broadcast_to(lax.axis_index("state"), (1, 1)).astype(jnp.int32)
    *ex, offt, sums, local_label, who, counts_row = prep(
        energies, offsets, counts.reshape(1, nk), labels.reshape(nblk, width // nblk), mine
    )
    groups = nblk // GROUP
    cuts = [groups * step // ITERS for step in range(ITERS + 1)]
    picked = []
    for step in range(ITERS):
        pair = paired(sums, partner(sums, state), nblk)
        parts = [pair, *others(pair, state)]
        picked.append(pick(energies, local_label, cuts[step], cuts[step + 1] - cuts[step], pair))
        out = update(parts, ex, offt, samp, picked[-1:])
        gathered = lax.all_to_all(out, "samp", 0, 0, tiled=True)
        if step < ITERS - 1:
            sums = denom(gathered, counts_row, ex, offt)
    keep, send, free = denom(gathered, counts_row, ex, offt, (local_label, who, *picked))
    pair = paired(keep, partner(send, state), nblk // 2)
    own, free = finish([pair, *others(pair, state)], free)
    own = join(own, partner(own, state), who)
    return free.reshape(nk), own.reshape(width)


def solution(mesh):
    return jax.shard_map(
        functools.partial(shards, mesh.shape["samp"], mesh.shape["state"]),
        mesh=mesh,
        in_specs=(P("state", "samp"), P("state", "samp"), P("state"), P("samp")),
        out_specs=(P("state"), P("samp")),
        check_vma=False,
    )
```

time: 142 us -> 118 us (0.83)
  Pallas kernels: 58.9 us -> 48.7 us
  waiting for transfers between devices: 22.4 us -> 12.3 us
  local copies, waits for them, and re-layouts: 2.98 us -> 0 us
  other arithmetic: 1.94 us -> 0 us
  starting transfers between devices: 21.4 us -> 23.2 us
    ppermute x16 -> x17, waiting for transfers between devices: 22.4 us -> 12.3 us  [shift_state(): return lax.ppermute(value, 'state', [(i, move(i)) for i in range(size)])]
    pallas_call x1, Pallas kernels: 18.9 us -> 11.4 us  [prep(): pl.pallas_call(prep_kernel, out_shape=(pltpu.VMEM((width // PIECES, nk),...]
    pallas_call x3, Pallas kernels: 12.2 us -> 8.52 us  [denom(): pl.pallas_call(last_kernel if extra else denom_kernel, out_shape=rows, in...]
    pallas_call x5 -> x9, Pallas kernels: 12.9 us -> 15.9 us  [the longest x3 13.7 us: pick(): pl.pallas_call(pick_kernel, grid=(count,), out_shape=jax.ShapeDtypeStruct...]
    unnamed x6 -> x0, local copies, waits for them, and re-layouts: 2.46 us -> none
    pallas_call x3, Pallas kernels: 14.9 us -> 13 us  [update(): pl.pallas_call(functools.partial(update_kernel, len(parts)), out_shape=ja...]
    ppermute x16 -> x17, starting transfers between devices: 21.4 us -> 23.2 us  [shift_state(): return lax.ppermute(value, 'state', [(i, move(i)) for i in range(size)])]
  transfers between devices with their start and end apart: 16 -> 17, of which waited for: 13 -> 11; matrix products, arithmetic and copies ran while one was open for 0% -> 0% of each run, Pallas kernels for 9% -> 12%
where the time goes in v2:
time: 118 us; the launch traced here: 117 us
  Pallas kernels  48.7 us (41%)
  blocking collectives  32.3 us (27%)
  starting transfers between devices  23.2 us (20%)
  waiting for transfers between devices  12.3 us (10%)
    all_to_all x3, blocking collectives, shards(): gathered = lax.all_to_all(out, 'samp', 0, 0, tiled=True)  32.3 us
    ppermute x17, starting transfers between devices, shift_state(): return lax.ppermute(value, 'state', [(i, move(i)) for i in range(size)])  23.2 us
    pallas_call x3, Pallas kernels, pick(): pl.pallas_call(pick_kernel, grid=(count,), out_shape=jax.ShapeDtypeStruct...  13.7 us
    pallas_call x3, Pallas kernels, update(): pl.pallas_call(functools.partial(update_kernel, len(parts)), out_shape=ja...  13 us
    ppermute x17, waiting for transfers between devices, shift_state(): return lax.ppermute(value, 'state', [(i, move(i)) for i in range(size)])  12.3 us
    pallas_call x1, Pallas kernels, prep(): pl.pallas_call(prep_kernel, out_shape=(pltpu.VMEM((width // PIECES, nk),...  11.4 us
    pallas_call x3, Pallas kernels, denom(): pl.pallas_call(last_kernel if extra else denom_kernel, out_shape=rows, in...  8.52 us
  transfers between devices with their start and end apart: 17, of which 11 were waited for; matrix products, arithmetic and copies ran while one was open for 0% of the time, Pallas kernels for 12%

profile of v2, /device:TPU:1, one launch (start us, length us, event | category | flops | bytes accessed | tf_op | source)
XLA Modules:
  0.0 117.4 jit_solution(12705101572387776642)
XLA Ops:
  0.6 11.4 %prep.1 = (f32[8192,512]{1,0:T(8,128)S(1)}, f32[8192,512]{1,0:T(8,128)S(1)}, f32[128,512]{1,0:T(8,128)S(1)}, f32[128,128]{1,0:T(8,128)S(1)}, s32[128,128]{1,0:T(...) custom-call(bf16[512,16384]{1,0:T(8,128)(2,1)} %e_ref.5, f32[512,128]{1,0:T(8,128)} %off_hbm.1, s32[1,512]{1,0:T(1,128)} %bitcast.7, ...), custom_call_target="tpu_custom_call" | custom-call | tf_op jit(solution)/shard_map/prep/pallas_call | solution.py:136
  12.0 1.5 %collective-permute-start = (f32[128,128]{1,0:T(8,128)S(1)}, f32[128,128]{1,0:T(8,128)S(1)}, u32[]{:S(2)}, u32[]{:S(2)}) collective-permute-start(f32[128,128]{1,0:T(8,128)S(1)} %get-tuple-element.14.a_ref), channel_id=1, source_target_pairs={{0,1},{1,0},{2,3},{3,2},{4,5},{5,4},{6,7},{7,6},{8,9},{9,8},{10,11... | collective-permute-start | bytes 196616 | tf_op jit(solution)/shard_map/ppermute | solution.py:398
  13.5 0.9 collective-permute-done.b_ref
  14.5 2.9 %collective-permute-start.3 = (f32[128,128]{1,0:T(8,128)S(1)}, f32[128,128]{1,0:T(8,128)S(1)}, u32[]{:S(2)}, u32[]{:S(2)}) collective-permute-start(f32[128,128]{1,0:T(8,128)S(1)} %pair.4._.refs_0_), channel_id=1, source_target_pairs={{0,6},{1,7},{2,0},{3,1},{4,2},{5,3},{6,4},{7,5},{8,14},{9,15},{10,... | collective-permute-start | bytes 196616 | tf_op jit(solution)/shard_map/ppermute | solution.py:398
  17.3 0.3 collective-permute-start.2
  17.7 0.7 collective-permute-start.1
  18.4 4.4 %pick.3.refs_7_.refs_5_ = f32[40,128]{1,0:T(8,128)S(1)} custom-call(bf16[512,16384]{1,0:T(8,128)(2,1)} %e_ref.5, s32[128,128]{1,0:T(8,128)S(1)} %get-tuple-element.18.label_ref.refs_3_, f32[128,128]{1,0:T(8,128)S(1)} %pair.4._.refs_0_), custom_call_target="tpu_custom_call" | custom-call | flops 7864320 | bytes 5242880 | tf_op jit(solution)/shard_map/pick/pallas_call | solution.py:179
  22.8 0.0 collective-permute-done.3.refs_3_
  22.8 0.0 collective-permute-done.2.refs_2_
  22.8 0.9 collective-permute-done.1.refs_1_
  23.8 4.3 %update.3 = f32[16,1,512]{2,1,0:T(1,128)S(1)} custom-call(f32[128,128]{1,0:T(8,128)S(1)} %pair.4._.refs_0_, f32[128,128]{1,0:T(8,128)S(1)} %collective-permute-done.1.refs_1_, f32[128,128]{1,0:T(8,128)S(1)} %collective-permute-done.2.refs_2_, f32[128,128]{1,0:T(8,128)S(1)} %collective-permute-done.3.refs_3_, ...), custom_call_target="tpu_custom_call" | custom-call | tf_op jit(solution)/shard_map/update/pallas_call | solution.py:240
  28.1 13.8 %all_to_all.15.gathered_ref = f32[16,1,512]{2,1,0:T(1,128)S(1)} all-to-all(f32[16,1,512]{2,1,0:T(1,128)S(1)} %update.3), channel_id=1, replica_groups=mesh['samp'=16,'state'=8] {'samp'}, dimensions={0} | all-to-all | bytes 65536 | tf_op jit(solution)/shard_map/all_to_all | solution.py:426
  41.9 2.6 %denom.2.a_ref = f32[128,128]{1,0:T(8,128)S(1)} custom-call(f32[16,1,512]{2,1,0:T(1,128)S(1)} %all_to_all.15.gathered_ref, s32[1,512]{1,0:T(1,128)S(1)} %get-tuple-element.19.counts_ref, f32[8192,512]{1,0:T(8,128)S(1)} %get-tuple-element.15.refs_4_.refs_0_, f32[8192,512]{1,0:T(8,128)S(1)} %get-tuple-element.16.refs_5_.refs_1_, ...), custom_call_target="tpu_custom_call" | custom-call | tf_op jit(solution)/shard_map/denom/pallas_call | solution.py:330
  44.5 2.5 %collective-permute-start.4 = (f32[128,128]{1,0:T(8,128)S(1)}, f32[128,128]{1,0:T(8,128)S(1)}, u32[]{:S(2)}, u32[]{:S(2)}) collective-permute-start(f32[128,128]{1,0:T(8,128)S(1)} %denom.2.a_ref), channel_id=1, source_target_pairs={{0,1},{1,0},{2,3},{3,2},{4,5},{5,4},{6,7},{7,6},{8,9},{9,8},{10,11... | collective-permute-start | bytes 196616 | tf_op jit(solution)/shard_map/ppermute | solution.py:398
  47.0 0.9 collective-permute-done.4.b_ref
  48.0 1.3 %collective-permute-start.7 = (f32[128,128]{1,0:T(8,128)S(1)}, f32[128,128]{1,0:T(8,128)S(1)}, u32[]{:S(2)}, u32[]{:S(2)}) collective-permute-start(f32[128,128]{1,0:T(8,128)S(1)} %pair.5._.refs_0_), channel_id=1, source_target_pairs={{0,6},{1,7},{2,0},{3,1},{4,2},{5,3},{6,4},{7,5},{8,14},{9,15},{10,... | collective-permute-start | bytes 196616 | tf_op jit(solution)/shard_map/ppermute | solution.py:398
  49.3 1.4 %collective-permute-start.6 = (f32[128,128]{1,0:T(8,128)S(1)}, f32[128,128]{1,0:T(8,128)S(1)}, u32[]{:S(2)}, u32[]{:S(2)}) collective-permute-start(f32[128,128]{1,0:T(8,128)S(1)} %pair.5._.refs_0_), channel_id=1, source_target_pairs={{0,4},{1,5},{2,6},{3,7},{4,0},{5,1},{6,2},{7,3},{8,12},{9,13},{10,... | collective-permute-start | bytes 196616 | tf_op jit(solution)/shard_map/ppermute | solution.py:398
  50.7 0.0 collective-permute-start.5
  50.7 4.4 %pick.4.refs_7_.refs_6_ = f32[40,128]{1,0:T(8,128)S(1)} custom-call(bf16[512,16384]{1,0:T(8,128)(2,1)} %e_ref.5, s32[128,128]{1,0:T(8,128)S(1)} %get-tuple-element.18.label_ref.refs_3_, f32[128,128]{1,0:T(8,128)S(1)} %pair.5._.refs_0_), custom_call_target="tpu_custom_call" | custom-call | flops 7864320 | bytes 5242880 | tf_op jit(solution)/shard_map/pick/pallas_call | solution.py:179
  55.2 0.0 collective-permute-done.7.refs_3_
  55.2 0.0 collective-permute-done.6.refs_2_
  55.2 0.6 collective-permute-done.5.refs_1_
  55.7 4.3 %update.4 = f32[16,1,512]{2,1,0:T(1,128)S(1)} custom-call(f32[128,128]{1,0:T(8,128)S(1)} %pair.5._.refs_0_, f32[128,128]{1,0:T(8,128)S(1)} %collective-permute-done.5.refs_1_, f32[128,128]{1,0:T(8,128)S(1)} %collective-permute-done.6.refs_2_, f32[128,128]{1,0:T(8,128)S(1)} %collective-permute-done.7.refs_3_, ...), custom_call_target="tpu_custom_call" | custom-call | tf_op jit(solution)/shard_map/update/pallas_call | solution.py:240
  60.1 9.2 %all_to_all.16.gathered_ref = f32[16,1,512]{2,1,0:T(1,128)S(1)} all-to-all(f32[16,1,512]{2,1,0:T(1,128)S(1)} %update.4), channel_id=1, replica_groups=mesh['samp'=16,'state'=8] {'samp'}, dimensions={0} | all-to-all | bytes 65536 | tf_op jit(solution)/shard_map/all_to_all | solution.py:426
  69.3 2.6 %denom.3.a_ref = f32[128,128]{1,0:T(8,128)S(1)} custom-call(f32[16,1,512]{2,1,0:T(1,128)S(1)} %all_to_all.16.gathered_ref, s32[1,512]{1,0:T(1,128)S(1)} %get-tuple-element.19.counts_ref, f32[8192,512]{1,0:T(8,128)S(1)} %get-tuple-element.15.refs_4_.refs_0_, f32[8192,512]{1,0:T(8,128)S(1)} %get-tuple-element.16.refs_5_.refs_1_, ...), custom_call_target="tpu_custom_call" | custom-call | tf_op jit(solution)/shard_map/denom/pallas_call | solution.py:330
  71.9 3.1 %collective-permute-start.8 = (f32[128,128]{1,0:T(8,128)S(1)}, f32[128,128]{1,0:T(8,128)S(1)}, u32[]{:S(2)}, u32[]{:S(2)}) collective-permute-start(f32[128,128]{1,0:T(8,128)S(1)} %denom.3.a_ref), channel_id=1, source_target_pairs={{0,1},{1,0},{2,3},{3,2},{4,5},{5,4},{6,7},{7,6},{8,9},{9,8},{10,11... | collective-permute-start | bytes 196616 | tf_op jit(solution)/shard_map/ppermute | solution.py:398
  75.0 0.9 collective-permute-done.8.b_ref
  75.9 2.0 %collective-permute-start.11 = (f32[128,128]{1,0:T(8,128)S(1)}, f32[128,128]{1,0:T(8,128)S(1)}, u32[]{:S(2)}, u32[]{:S(2)}) collective-permute-start(f32[128,128]{1,0:T(8,128)S(1)} %pair.6._.refs_0_), channel_id=1, source_target_pairs={{0,6},{1,7},{2,0},{3,1},{4,2},{5,3},{6,4},{7,5},{8,14},{9,15},{10,... | collective-permute-start | bytes 196616 | tf_op jit(solution)/shard_map/ppermute | solution.py:398
  77.9 0.3 collective-permute-start.10
  78.3 0.3 collective-permute-start.9
  78.6 4.8 %pick.5.refs_7_ = f32[48,128]{1,0:T(8,128)S(1)} custom-call(bf16[512,16384]{1,0:T(8,128)(2,1)} %e_ref.5, s32[128,128]{1,0:T(8,128)S(1)} %get-tuple-element.18.label_ref.refs_3_, f32[128,128]{1,0:T(8,128)S(1)} %pair.6._.refs_0_), custom_call_target="tpu_custom_call" | custom-call | flops 9437184 | bytes 6291456 | tf_op jit(solution)/shard_map/pick/pallas_call | solution.py:179
  83.4 0.0 collective-permute-done.11.refs_3_
  83.4 0.0 collective-permute-done.10.refs_2_
  83.5 0.9 collective-permute-done.9.refs_1_
  84.3 4.3 %update.5 = f32[16,1,512]{2,1,0:T(1,128)S(1)} custom-call(f32[128,128]{1,0:T(8,128)S(1)} %pair.6._.refs_0_, f32[128,128]{1,0:T(8,128)S(1)} %collective-permute-done.9.refs_1_, f32[128,128]{1,0:T(8,128)S(1)} %collective-permute-done.10.refs_2_, f32[128,128]{1,0:T(8,128)S(1)} %collective-permute-done.11.refs_3_, ...), custom_call_target="tpu_custom_call" | custom-call | tf_op jit(solution)/shard_map/update/pallas_call | solution.py:240
  88.6 9.2 %all_to_all.17.gathered_ref = f32[16,1,512]{2,1,0:T(1,128)S(1)} all-to-all(f32[16,1,512]{2,1,0:T(1,128)S(1)} %update.5), channel_id=1, replica_groups=mesh['samp'=16,'state'=8] {'samp'}, dimensions={0} | all-to-all | bytes 65536 | tf_op jit(solution)/shard_map/all_to_all | solution.py:426
  97.9 3.4 %last.1 = (f32[136,128]{1,0:T(8,128)S(1)}, f32[136,128]{1,0:T(8,128)S(1)}, f32[1,512]{1,0:T(1,128)S(1)}) custom-call(f32[16,1,512]{2,1,0:T(1,128)S(1)} %all_to_all.17.gathered_ref, s32[1,512]{1,0:T(1,128)S(1)} %get-tuple-element.19.counts_ref, f32[8192,512]{1,0:T(8,128)S(1)} %get-tuple-element.15.refs_4_.refs_0_, ...), custom_call_target="tpu_custom_call" | custom-call | tf_op jit(solution)/shard_map/last/pallas_call | solution.py:330
  101.3 2.5 %collective-permute-start.12 = (f32[136,128]{1,0:T(8,128)S(1)}, f32[136,128]{1,0:T(8,128)S(1)}, u32[]{:S(2)}, u32[]{:S(2)}) collective-permute-start(f32[136,128]{1,0:T(8,128)S(1)} %get-tuple-element.22), channel_id=1, source_target_pairs={{0,1},{1,0},{2,3},{3,2},{4,5},{5,4},{6,7},{7,6},{8,9},{9,8},{10,11... | collective-permute-start | bytes 208904 | tf_op jit(solution)/shard_map/ppermute | solution.py:398
  103.8 0.9 collective-permute-done.12.b_ref
  104.7 1.8 %collective-permute-start.15 = (f32[136,128]{1,0:T(8,128)S(1)}, f32[136,128]{1,0:T(8,128)S(1)}, u32[]{:S(2)}, u32[]{:S(2)}) collective-permute-start(f32[136,128]{1,0:T(8,128)S(1)} %pair.7.refs_0_), channel_id=1, source_target_pairs={{0,6},{1,7},{2,0},{3,1},{4,2},{5,3},{6,4},{7,5},{8,14},{9,15},{10,... | collective-permute-start | bytes 208904 | tf_op jit(solution)/shard_map/ppermute | solution.py:398
  106.5 1.4 %collective-permute-start.14 = (f32[136,128]{1,0:T(8,128)S(1)}, f32[136,128]{1,0:T(8,128)S(1)}, u32[]{:S(2)}, u32[]{:S(2)}) collective-permute-start(f32[136,128]{1,0:T(8,128)S(1)} %pair.7.refs_0_), channel_id=1, source_target_pairs={{0,4},{1,5},{2,6},{3,7},{4,0},{5,1},{6,2},{7,3},{8,12},{9,13},{10,... | collective-permute-start | bytes 208904 | tf_op jit(solution)/shard_map/ppermute | solution.py:398
  107.9 0.0 collective-permute-start.13
  107.9 0.1 collective-permute-done.15.refs_3_
  108.0 3.2 %collective-permute-done.14.refs_2_ = f32[136,128]{1,0:T(8,128)S(1)} collective-permute-done((f32[136,128]{1,0:T(8,128)S(1)}, f32[136,128]{1,0:T(8,128)S(1)}, u32[]{:S(2)}, u32[]{:S(2)}) %collective-permute-start.14) | collective-permute-done | bytes 69664 | tf_op jit(solution)/shard_map/ppermute | solution.py:398
  111.2 2.2 %collective-permute-done.13.refs_1_ = f32[136,128]{1,0:T(8,128)S(1)} collective-permute-done((f32[136,128]{1,0:T(8,128)S(1)}, f32[136,128]{1,0:T(8,128)S(1)}, u32[]{:S(2)}, u32[]{:S(2)}) %collective-permute-start.13) | collective-permute-done | bytes 69664 | tf_op jit(solution)/shard_map/ppermute | solution.py:398
  113.4 0.7 finish.1
  114.0 1.1 collective-permute-start.16
  115.1 0.9 collective-permute-done.16.theirs_ref
  116.0 1.4 %join.1 = f32[128,128]{1,0:T(8,128)} custom-call(f32[64,128]{1,0:T(8,128)S(1)} %get-tuple-element.25.mine_ref, f32[64,128]{1,0:T(8,128)S(1)} %collective-permute-done.16.theirs_ref, s32[1,1]{1,0:T(1,128)} %get-tuple-element.20.refs_4_.who_ref), custom_call_target="tpu_custom_call" | custom-call | tf_op jit(solution)/shard_map/join/pallas_call | solution.py:387
  (4 shorter events, 0.2 us)
Async XLA Ops:
  12.0 2.4 %collective-permute-start = (f32[128,128]{1,0:T(8,128)S(1)}, f32[128,128]{1,0:T(8,128)S(1)}, u32[]{:S(2)}, u32[]{:S(2)}) collective-permute-start(f32[128,128]{1,0:T(8,128)S(1)} %get-tuple-element.14.a_ref), channel_id=1, source_target_pairs={{0,1},{1,0},{2,3},{3,2},{4,5},{5,4},{6,7},{7,6},{8,9},{9,8},{10,11... | collective-permute-start | bytes 196616 | tf_op jit(solution)/shard_map/ppermute | solution.py:398
  14.5 8.4 %collective-permute-start.3 = (f32[128,128]{1,0:T(8,128)S(1)}, f32[128,128]{1,0:T(8,128)S(1)}, u32[]{:S(2)}, u32[]{:S(2)}) collective-permute-start(f32[128,128]{1,0:T(8,128)S(1)} %pair.4._.refs_0_), channel_id=1, source_target_pairs={{0,6},{1,7},{2,0},{3,1},{4,2},{5,3},{6,4},{7,5},{8,14},{9,15},{10,... | collective-permute-start | bytes 196616 | tf_op jit(solution)/shard_map/ppermute | solution.py:398
  17.3 5.5 %collective-permute-start.2 = (f32[128,128]{1,0:T(8,128)S(1)}, f32[128,128]{1,0:T(8,128)S(1)}, u32[]{:S(2)}, u32[]{:S(2)}) collective-permute-start(f32[128,128]{1,0:T(8,128)S(1)} %pair.4._.refs_0_), channel_id=1, source_target_pairs={{0,4},{1,5},{2,6},{3,7},{4,0},{5,1},{6,2},{7,3},{8,12},{9,13},{10,... | collective-permute-start | bytes 196616 | tf_op jit(solution)/shard_map/ppermute | solution.py:398
  17.7 6.1 %collective-permute-start.1 = (f32[128,128]{1,0:T(8,128)S(1)}, f32[128,128]{1,0:T(8,128)S(1)}, u32[]{:S(2)}, u32[]{:S(2)}) collective-permute-start(f32[128,128]{1,0:T(8,128)S(1)} %pair.4._.refs_0_), channel_id=1, source_target_pairs={{0,2},{1,3},{2,4},{3,5},{4,6},{5,7},{6,0},{7,1},{8,10},{9,11},{10,... | collective-permute-start | bytes 196616 | tf_op jit(solution)/shard_map/ppermute | solution.py:398
  44.5 3.4 %collective-permute-start.4 = (f32[128,128]{1,0:T(8,128)S(1)}, f32[128,128]{1,0:T(8,128)S(1)}, u32[]{:S(2)}, u32[]{:S(2)}) collective-permute-start(f32[128,128]{1,0:T(8,128)S(1)} %denom.2.a_ref), channel_id=1, source_target_pairs={{0,1},{1,0},{2,3},{3,2},{4,5},{5,4},{6,7},{7,6},{8,9},{9,8},{10,11... | collective-permute-start | bytes 196616 | tf_op jit(solution)/shard_map/ppermute | solution.py:398
  48.0 7.2 %collective-permute-start.7 = (f32[128,128]{1,0:T(8,128)S(1)}, f32[128,128]{1,0:T(8,128)S(1)}, u32[]{:S(2)}, u32[]{:S(2)}) collective-permute-start(f32[128,128]{1,0:T(8,128)S(1)} %pair.5._.refs_0_), channel_id=1, source_target_pairs={{0,6},{1,7},{2,0},{3,1},{4,2},{5,3},{6,4},{7,5},{8,14},{9,15},{10,... | collective-permute-start | bytes 196616 | tf_op jit(solution)/shard_map/ppermute | solution.py:398
  49.3 5.9 %collective-permute-start.6 = (f32[128,128]{1,0:T(8,128)S(1)}, f32[128,128]{1,0:T(8,128)S(1)}, u32[]{:S(2)}, u32[]{:S(2)}) collective-permute-start(f32[128,128]{1,0:T(8,128)S(1)} %pair.5._.refs_0_), channel_id=1, source_target_pairs={{0,4},{1,5},{2,6},{3,7},{4,0},{5,1},{6,2},{7,3},{8,12},{9,13},{10,... | collective-permute-start | bytes 196616 | tf_op jit(solution)/shard_map/ppermute | solution.py:398
  50.7 5.0 %collective-permute-start.5 = (f32[128,128]{1,0:T(8,128)S(1)}, f32[128,128]{1,0:T(8,128)S(1)}, u32[]{:S(2)}, u32[]{:S(2)}) collective-permute-start(f32[128,128]{1,0:T(8,128)S(1)} %pair.5._.refs_0_), channel_id=1, source_target_pairs={{0,2},{1,3},{2,4},{3,5},{4,6},{5,7},{6,0},{7,1},{8,10},{9,11},{10,... | collective-permute-start | bytes 196616 | tf_op jit(solution)/shard_map/ppermute | solution.py:398
  71.9 4.0 %collective-permute-start.8 = (f32[128,128]{1,0:T(8,128)S(1)}, f32[128,128]{1,0:T(8,128)S(1)}, u32[]{:S(2)}, u32[]{:S(2)}) collective-permute-start(f32[128,128]{1,0:T(8,128)S(1)} %denom.3.a_ref), channel_id=1, source_target_pairs={{0,1},{1,0},{2,3},{3,2},{4,5},{5,4},{6,7},{7,6},{8,9},{9,8},{10,11... | collective-permute-start | bytes 196616 | tf_op jit(solution)/shard_map/ppermute | solution.py:398
  75.9 7.5 %collective-permute-start.11 = (f32[128,128]{1,0:T(8,128)S(1)}, f32[128,128]{1,0:T(8,128)S(1)}, u32[]{:S(2)}, u32[]{:S(2)}) collective-permute-start(f32[128,128]{1,0:T(8,128)S(1)} %pair.6._.refs_0_), channel_id=1, source_target_pairs={{0,6},{1,7},{2,0},{3,1},{4,2},{5,3},{6,4},{7,5},{8,14},{9,15},{10,... | collective-permute-start | bytes 196616 | tf_op jit(solution)/shard_map/ppermute | solution.py:398
  77.9 5.5 %collective-permute-start.10 = (f32[128,128]{1,0:T(8,128)S(1)}, f32[128,128]{1,0:T(8,128)S(1)}, u32[]{:S(2)}, u32[]{:S(2)}) collective-permute-start(f32[128,128]{1,0:T(8,128)S(1)} %pair.6._.refs_0_), channel_id=1, source_target_pairs={{0,4},{1,5},{2,6},{3,7},{4,0},{5,1},{6,2},{7,3},{8,12},{9,13},{10,... | collective-permute-start | bytes 196616 | tf_op jit(solution)/shard_map/ppermute | solution.py:398
  78.3 6.1 %collective-permute-start.9 = (f32[128,128]{1,0:T(8,128)S(1)}, f32[128,128]{1,0:T(8,128)S(1)}, u32[]{:S(2)}, u32[]{:S(2)}) collective-permute-start(f32[128,128]{1,0:T(8,128)S(1)} %pair.6._.refs_0_), channel_id=1, source_target_pairs={{0,2},{1,3},{2,4},{3,5},{4,6},{5,7},{6,0},{7,1},{8,10},{9,11},{10,... | collective-permute-start | bytes 196616 | tf_op jit(solution)/shard_map/ppermute | solution.py:398
  101.3 3.4 %collective-permute-start.12 = (f32[136,128]{1,0:T(8,128)S(1)}, f32[136,128]{1,0:T(8,128)S(1)}, u32[]{:S(2)}, u32[]{:S(2)}) collective-permute-start(f32[136,128]{1,0:T(8,128)S(1)} %get-tuple-element.22), channel_id=1, source_target_pairs={{0,1},{1,0},{2,3},{3,2},{4,5},{5,4},{6,7},{7,6},{8,9},{9,8},{10,11... | collective-permute-start | bytes 208904 | tf_op jit(solution)/shard_map/ppermute | solution.py:398
  104.7 3.2 %collective-permute-start.15 = (f32[136,128]{1,0:T(8,128)S(1)}, f32[136,128]{1,0:T(8,128)S(1)}, u32[]{:S(2)}, u32[]{:S(2)}) collective-permute-start(f32[136,128]{1,0:T(8,128)S(1)} %pair.7.refs_0_), channel_id=1, source_target_pairs={{0,6},{1,7},{2,0},{3,1},{4,2},{5,3},{6,4},{7,5},{8,14},{9,15},{10,... | collective-permute-start | bytes 208904 | tf_op jit(solution)/shard_map/ppermute | solution.py:398
  106.5 4.7 %collective-permute-start.14 = (f32[136,128]{1,0:T(8,128)S(1)}, f32[136,128]{1,0:T(8,128)S(1)}, u32[]{:S(2)}, u32[]{:S(2)}) collective-permute-start(f32[136,128]{1,0:T(8,128)S(1)} %pair.7.refs_0_), channel_id=1, source_target_pairs={{0,4},{1,5},{2,6},{3,7},{4,0},{5,1},{6,2},{7,3},{8,12},{9,13},{10,... | collective-permute-start | bytes 208904 | tf_op jit(solution)/shard_map/ppermute | solution.py:398
  107.9 5.5 %collective-permute-start.13 = (f32[136,128]{1,0:T(8,128)S(1)}, f32[136,128]{1,0:T(8,128)S(1)}, u32[]{:S(2)}, u32[]{:S(2)}) collective-permute-start(f32[136,128]{1,0:T(8,128)S(1)} %pair.7.refs_0_), channel_id=1, source_target_pairs={{0,2},{1,3},{2,4},{3,5},{4,6},{5,7},{6,0},{7,1},{8,10},{9,11},{10,... | collective-permute-start | bytes 208904 | tf_op jit(solution)/shard_map/ppermute | solution.py:398
  114.0 1.9 %collective-permute-start.16 = (f32[64,128]{1,0:T(8,128)S(1)}, f32[64,128]{1,0:T(8,128)S(1)}, u32[]{:S(2)}, u32[]{:S(2)}) collective-permute-start(f32[64,128]{1,0:T(8,128)S(1)} %get-tuple-element.25.mine_ref), channel_id=1, source_target_pairs={{0,1},{1,0},{2,3},{3,2},{4,5},{5,4},{6,7},{7,6},{8,9},{9,8},{10,11... | collective-permute-start | bytes 98312 | tf_op jit(solution)/shard_map/ppermute | solution.py:398
